TPU v7x, 256 devices: a whole 4x4x8 slice. The times are simulated.
256 devices in a mesh: span: 32 (over x, z), plane: 8 (over y, core).
Axes of the slice: x: 4, y: 4, z: 8, core: 2. Of those that a mesh axis runs over, the one named last changes fastest.
Arguments:
- rhs: float32 [80, 8192], P(None, ('span', 'plane')), may hold values from -6 to 6
- blocks: float32 [8192, 70400], P(('span', 'plane')), as said below
- columns: int32 [11, 8192], P(None, ('span', 'plane')), may hold values from 0 to 8191, as said below
- line_slot: int32 [256, 32], P(('span', 'plane')), may hold values from 0 to 31, each once within a row
- line_lower: float32 [8192, 6400], P(('span', 'plane')), may hold values from -0.2 to 0.2
- line_upper: float32 [8192, 6400], P(('span', 'plane')), may hold values from -0.2 to 0.2
- pivot_inv: float32 [8192, 6400], P(('span', 'plane')), as said below
Outputs:
- solution: float32 [80, 8192], P(None, ('span', 'plane'))
- residual: float32 [80, 8192], P(None, ('span', 'plane'))
Inputs may be any that keep to these rules, and one draw needn't show every extreme that they name: columns[0, i] = i; the other columns name faces on the device itself, on the devices one step along span (wrapping) or one step along plane (not wrapping). Blocks 1 to 4 name faces on the span devices after and before and the plane devices after and before, or on the device itself where no such plane device exists. pivot_inv is a diagonal with entries between about 0.5 and 2.0 plus a full-rank off-diagonal part of small entries. `blocks`: block 0 of every row has an added diagonal of 1 to about 4.06.
All inputs are finite; a program needn't handle non-finite values.
Results may differ from a plain program's by a relative error of at most 0.0065.
Values sent between devices are 32-bit elements; how exact they have to be, the bound alone decides.
A program may use at most 128 MiB of HBM per device.

v0:
```python
import jax
import jax.numpy as jnp
from jax import lax
from jax.sharding import PartitionSpec as P

ITERS = 3
P_SIZE = 2


HIGH = lax.Precision.HIGHEST


def with_halo(x, sides, width, wrap):
    for axis, dim in sides:
        size, length = (lax.axis_size(axis), x.shape[dim])
        up = [(i, (i + 1) % size) for i in range(size if wrap else size - 1)]
        down = [(j, i) for i, j in up]
        last = lax.slice_in_dim(x, length - width, length, axis=dim)
        first = lax.slice_in_dim(x, 0, width, axis=dim)
        before = lax.ppermute(last, axis, up)
        after = lax.ppermute(first, axis, down)
        x = jnp.concatenate([before, x, after], axis=dim)
    return x


def small_solve(factor, target):
    extent = target.shape[0]
    forward_vals = []
    for row in range(extent):
        running = target[row]
        for inner in range(row):
            running = running - factor[row, inner] * forward_vals[inner]
        forward_vals.append(running / factor[row, row])
    backward_vals = [None] * extent
    for row in reversed(range(extent)):
        running = forward_vals[row]
        for inner in range(row + 1, extent):
            running = running - factor[inner, row] * backward_vals[inner]
        backward_vals[row] = running / factor[row, row]
    return jnp.stack(backward_vals)


def to_sequence(factor_rows, nlines, length, width):
    return jnp.swapaxes(factor_rows.reshape(nlines, length, width, width), 0, 1)


def line_solve(rhs_lines, lseq, useq, pseq):
    rseq = jnp.moveaxis(rhs_lines, 2, 0)

    def forward(prev, items):
        right, low = items
        cur = right - jnp.einsum("mab,bm->am", low, prev, precision=HIGH)
        return (cur, cur)

    start = jnp.zeros(rseq.shape[1:], jnp.float32)
    _, yseq = lax.scan(forward, start, (rseq, lseq))

    def backward(nxt, items):
        yval, upp, piv = items
        inner = yval - jnp.einsum("mab,bm->am", upp, nxt, precision=HIGH)
        cur = jnp.einsum("mab,bm->am", piv, inner, precision=HIGH)
        return (cur, cur)

    _, zseq = lax.scan(backward, start, (yseq, useq, pseq), reverse=True)
    return jnp.moveaxis(zseq, 0, 2)


def on_device(rhs, blocks, columns, line_slot, line_lower, line_upper, pivot_inv):
    width = rhs.shape[0]
    nfaces = rhs.shape[1]
    nblocks = columns.shape[0]
    nspan = lax.axis_size("span")
    nplane = lax.axis_size("plane")
    my_span = lax.axis_index("span")
    my_plane = lax.axis_index("plane")
    device_of = columns // nfaces
    span_of = device_of // nplane
    plane_of = device_of % nplane
    dspan = (span_of - my_span + 1 + nspan) % nspan - 1
    dplane = plane_of - my_plane
    selector = jnp.where(
        dspan == -1,
        1,
        jnp.where(dspan == 1, 2, jnp.where(dplane == -1, 3, jnp.where(dplane == 1, 4, 0))),
    )
    position = selector * nfaces + columns % nfaces
    slot = line_slot[0]
    lines_group = nfaces // P_SIZE
    owned = lines_group // nplane
    length = P_SIZE * nplane
    lower = to_sequence(line_lower, owned, length, width)
    upper = to_sequence(line_upper, owned, length, width)
    pivot = to_sequence(pivot_inv, owned, length, width)
    shaped_blocks = blocks.reshape(nfaces, nblocks, width, width)

    def apply_a(vec):
        shaped = vec.reshape(width, 1, 1, nfaces)
        span_side = with_halo(shaped, (("span", 1),), 1, True)
        plane_side = with_halo(shaped, (("plane", 2),), 1, False)
        below = plane_side[:, 0, 0]
        above = plane_side[:, 0, 2]
        table = jnp.concatenate([vec, span_side[:, 0, 0], span_side[:, 2, 0], below, above], axis=1)
        picked = table[:, position]
        return jnp.einsum("ikab,bki->ai", shaped_blocks, picked, precision=HIGH)

    def apply_m(vec):
        pieces = vec[:, slot].reshape(width, lines_group, P_SIZE)
        whole = lax.all_to_all(pieces, "plane", split_axis=1, concat_axis=2, tiled=True)
        solved = line_solve(whole, lower, upper, pivot)
        every = None
        back = lax.all_to_all(solved, "plane", split_axis=2, concat_axis=1, tiled=True)
        return (jnp.zeros_like(vec).at[:, slot].set(back.reshape(width, nfaces)), every)

    beta = jnp.sqrt(lax.psum(jnp.sum(rhs * rhs), ("span", "plane")) + 1e-06)
    basis = [rhs / beta]
    hcols = []
    for step in range(ITERS):
        precond, lines_held = apply_m(basis[step])
        wvec = apply_a(precond)
        stacked = jnp.stack(basis)
        local_proj = jnp.einsum("jai,ai->j", stacked, wvec, precision=HIGH)
        hvals = lax.psum(local_proj, ("span", "plane"))
        wvec = wvec - jnp.einsum("j,jai->ai", hvals, stacked, precision=HIGH)
        square = lax.psum(jnp.sum(wvec * wvec), ("span", "plane"))
        hnext = jnp.sqrt(square + 1e-06)
        basis.append(wvec / hnext)
        hcols.append(
            jnp.concatenate([hvals, hnext[None], jnp.zeros((ITERS - step - 1,), jnp.float32)])
        )
    hmat = jnp.stack(hcols, axis=1)
    gram_mat = jnp.dot(hmat.T, hmat, precision=HIGH)
    target = beta * hmat[0]
    factor = jnp.linalg.cholesky(gram_mat)
    coef = small_solve(factor, target)
    update = jnp.einsum("j,jai->ai", coef, jnp.stack(basis[:ITERS]), precision=HIGH)
    solution, lines_final = apply_m(update)
    residual = rhs - apply_a(solution)
    return (solution, residual)


def solution(mesh):
    return jax.shard_map(
        on_device,
        mesh=mesh,
        in_specs=(
            P(None, ("span", "plane")),
            P(("span", "plane"), None),
            P(None, ("span", "plane")),
            P(("span", "plane"), None),
            P(("span", "plane"), None),
            P(("span", "plane"), None),
            P(("span", "plane"), None),
        ),
        out_specs=(P(None, ("span", "plane")), P(None, ("span", "plane"))),
        check_vma=False,
    )
```

profile of v0, /device:TPU:1, one launch (start us, length us, event | category | flops | bytes accessed | tf_op | source)
XLA Modules:
  0.0 897.0 jit_solution(2736150727583213987)
XLA Ops:
  2.6 81.4 %psum.49 = f32[]{:T(128)} all-reduce(f32[]{:T(128)} %multiply_reduce_fusion.4), channel_id=1, replica_groups=mesh['span'=32,'plane'=8] {'span','plane'}, use_global_device_ids=true, to_apply=%region_1.2 | all-reduce | flops 1 | bytes 8 | tf_op jit(solution)/shard_map/psum | solution.py:114
  86.6 4.2 all-to-all-start
  100.7 18.5 %while.120 = (s32[]{:T(128)}, f32[80,2]{0,1:T(2,128)S(1)}, f32[16,80,2]{1,2,0:T(2,128)S(1)}, f32[16,80,2]{1,2,0:T(2,128)S(1)}, f32[16,2,80,80]{3,2,1,0:T(8,128)}, /*index=5*/s32[]{:T(128)}, s32[]{:T(128)}) while((s32[]{:T(128)}, f32[80,2]{0,1:T(2,128)S(1)}, f32[16,80,2]{1,2,0:T(2,128)S(1)}, f32[16,80,2]{1,2,0:T(2,128)S(1)}, ...), condition=%wide.region_3.4_spmd.clone, body=%wide.region_2.3_spmd.clone.sunk | while | flops 153923 | bytes 89179 | solution.py:56
  119.9 17.2 %while.116 = (s32[]{:T(128)}, f32[80,2]{0,1:T(2,128)S(1)}, f32[16,80,2]{1,2,0:T(2,128)}, f32[16,80,2]{1,2,0:T(2,128)S(1)}, f32[16,2,80,80]{3,2,1,0:T(8,128)S(1)}...) while((s32[]{:T(128)}, f32[80,2]{0,1:T(2,128)S(1)}, f32[16,80,2]{1,2,0:T(2,128)}, ...), condition=%wide.region_5.6_spmd, body=%wide.region_4.5_spmd.sunk | while | flops 307363 | bytes 170865 | solution.py:64
  137.1 4.8 all-to-all-start.1
  141.9 14.6 %reshape.115 = f32[32,11,80,80]{3,2,1,0:T(8,128)} reshape(f32[32,70400]{1,0:T(8,128)} %param.24) | data formatting | bytes 18022400 | tf_op jit(solution)/shard_map/reshape | solution.py:94
  157.9 4.2 collective-permute-start.1
  162.1 4.1 collective-permute-start.2
  172.4 16.1 %fusion.62 = f32[32,1,80,1]{2,1,3,0:T(1,128)S(1)} fusion(f32[32,11,80,80]{3,2,1,0:T(8,128)} %reshape.115, f32[80,11,32,1]{0,2,1,3:T(8,128)S(1)} %bitcast.520), kind=kOutput, calls=%fused_computation.96 | convolution fusion | flops 27033600 | bytes 9134080 | tf_op jit(solution)/shard_map/ikab,bki->ai/dot_general | solution.py:104
  189.1 73.3 %psum.50 = f32[1]{0:T(128)} all-reduce(f32[1]{0:T(128)} %bitcast.87), channel_id=1, replica_groups=mesh['span'=32,'plane'=8] {'span','plane'}, use_global_device_ids=true, to_apply=%region_7.8 | all-reduce | flops 1 | bytes 8 | tf_op jit(solution)/shard_map/psum | solution.py:122
  263.6 73.4 %psum.51 = f32[]{:T(128)} all-reduce(f32[]{:T(128)} %multiply_reduce_fusion.3), channel_id=1, replica_groups=mesh['span'=32,'plane'=8] {'span','plane'}, use_global_device_ids=true, to_apply=%region_9.10 | all-reduce | flops 1 | bytes 8 | tf_op jit(solution)/shard_map/psum | solution.py:124
  343.4 4.7 all-to-all-done.2
  348.1 18.5 %while.121 = (s32[]{:T(128)}, f32[80,2]{0,1:T(2,128)S(1)}, f32[16,80,2]{1,2,0:T(2,128)S(1)}, f32[16,80,2]{1,2,0:T(2,128)S(1)}, f32[16,2,80,80]{3,2,1,0:T(8,128)}, /*index=5*/s32[]{:T(128)}, s32[]{:T(128)}) while((s32[]{:T(128)}, f32[80,2]{0,1:T(2,128)S(1)}, f32[16,80,2]{1,2,0:T(2,128)S(1)}, f32[16,80,2]{1,2,0:T(2,128)S(1)}, ...), condition=%wide.region_11.12_spmd.clone, body=%wide.region_10.11_spmd.clone.sunk | while | flops 153923 | bytes 89179 | solution.py:56
  367.2 17.2 %while.117 = (s32[]{:T(128)}, f32[80,2]{0,1:T(2,128)S(1)}, f32[16,80,2]{1,2,0:T(2,128)}, f32[16,80,2]{1,2,0:T(2,128)S(1)}, f32[16,2,80,80]{3,2,1,0:T(8,128)S(1)}...) while((s32[]{:T(128)}, f32[80,2]{0,1:T(2,128)S(1)}, f32[16,80,2]{1,2,0:T(2,128)}, ...), condition=%wide.region_13.14_spmd, body=%wide.region_12.13_spmd.sunk | while | flops 307363 | bytes 170865 | solution.py:64
  384.4 3.9 all-to-all-start.3
  388.4 4.7 all-to-all-done.3
  408.1 16.1 %fusion.60 = f32[32,1,80,1]{2,1,3,0:T(1,128)S(1)} fusion(f32[32,11,80,80]{3,2,1,0:T(8,128)} %reshape.115, f32[80,11,32,1]{0,2,1,3:T(8,128)S(1)} %bitcast.521), kind=kOutput, calls=%fused_computation.94 | convolution fusion | flops 27033600 | bytes 9134080 | tf_op jit(solution)/shard_map/ikab,bki->ai/dot_general | solution.py:104
  424.6 72.7 %psum.52 = f32[2]{0:T(128)S(1)} all-reduce(f32[2]{0:T(128)S(1)} %convolution_bitcast_fusion.1), channel_id=1, replica_groups=mesh['span'=32,'plane'=8] {'span','plane'}, use_global_device_ids=true, to_apply=%region_15.16 | all-reduce | flops 2 | bytes 16 | tf_op jit(solution)/shard_map/psum | solution.py:122
  498.1 73.5 %psum.53 = f32[]{:T(128)} all-reduce(f32[]{:T(128)} %get-tuple-element.862), channel_id=1, replica_groups=mesh['span'=32,'plane'=8] {'span','plane'}, use_global_device_ids=true, to_apply=%region_17.18 | all-reduce | flops 1 | bytes 8 | tf_op jit(solution)/shard_map/psum | solution.py:124
  577.5 4.7 all-to-all-done.4
  582.1 18.5 %while.122 = (s32[]{:T(128)}, f32[80,2]{0,1:T(2,128)S(1)}, f32[16,80,2]{1,2,0:T(2,128)S(1)}, f32[16,80,2]{1,2,0:T(2,128)S(1)}, f32[16,2,80,80]{3,2,1,0:T(8,128)}, /*index=5*/s32[]{:T(128)}, s32[]{:T(128)}) while((s32[]{:T(128)}, f32[80,2]{0,1:T(2,128)S(1)}, f32[16,80,2]{1,2,0:T(2,128)S(1)}, f32[16,80,2]{1,2,0:T(2,128)S(1)}, ...), condition=%wide.region_19.20_spmd.clone, body=%wide.region_18.19_spmd.clone.sunk | while | flops 153923 | bytes 89179 | solution.py:56
  601.3 17.2 %while.118 = (s32[]{:T(128)}, f32[80,2]{0,1:T(2,128)S(1)}, f32[16,80,2]{1,2,0:T(2,128)}, f32[16,80,2]{1,2,0:T(2,128)S(1)}, f32[16,2,80,80]{3,2,1,0:T(8,128)S(1)}...) while((s32[]{:T(128)}, f32[80,2]{0,1:T(2,128)S(1)}, f32[16,80,2]{1,2,0:T(2,128)}, ...), condition=%wide.region_21.22_spmd, body=%wide.region_20.21_spmd.sunk | while | flops 307363 | bytes 170865 | solution.py:64
  618.5 3.9 all-to-all-start.5
  622.4 4.7 all-to-all-done.5
  642.2 16.1 %fusion.58 = f32[32,1,80,1]{2,1,3,0:T(1,128)S(1)} fusion(f32[32,11,80,80]{3,2,1,0:T(8,128)} %reshape.115, f32[80,11,32,1]{0,2,1,3:T(8,128)S(1)} %bitcast.522), kind=kOutput, calls=%fused_computation.92 | convolution fusion | flops 27033600 | bytes 9134080 | tf_op jit(solution)/shard_map/ikab,bki->ai/dot_general | solution.py:104
  659.4 72.7 %psum.54 = f32[3]{0:T(128)S(1)} all-reduce(f32[3]{0:T(128)S(1)} %convolution_bitcast_fusion), channel_id=1, replica_groups=mesh['span'=32,'plane'=8] {'span','plane'}, use_global_device_ids=true, to_apply=%region_23.24 | all-reduce | flops 3 | bytes 24 | tf_op jit(solution)/shard_map/psum | solution.py:122
  733.0 73.5 %psum.55 = f32[]{:T(128)} all-reduce(f32[]{:T(128)} %multiply_reduce_fusion.1), channel_id=1, replica_groups=mesh['span'=32,'plane'=8] {'span','plane'}, use_global_device_ids=true, to_apply=%region_25.26 | all-reduce | flops 1 | bytes 8 | tf_op jit(solution)/shard_map/psum | solution.py:124
  825.5 4.7 all-to-all-done.6
  830.2 18.5 %while.123 = (s32[]{:T(128)}, f32[80,2]{0,1:T(2,128)S(1)}, f32[16,80,2]{1,2,0:T(2,128)S(1)}, f32[16,80,2]{1,2,0:T(2,128)S(1)}, f32[16,2,80,80]{3,2,1,0:T(8,128)}, /*index=5*/s32[]{:T(128)}, s32[]{:T(128)}) while((s32[]{:T(128)}, f32[80,2]{0,1:T(2,128)S(1)}, f32[16,80,2]{1,2,0:T(2,128)S(1)}, f32[16,80,2]{1,2,0:T(2,128)S(1)}, ...), condition=%wide.region_29.30_spmd.clone, body=%wide.region_28.29_spmd.clone.sunk | while | flops 153923 | bytes 89179 | solution.py:56
  848.7 8.4 while.119
  857.0 7.7 all_to_all.132
  879.9 16.1 %fusion.56 = f32[32,1,80,1]{2,1,3,0:T(1,128)S(1)} fusion(f32[32,11,80,80]{3,2,1,0:T(8,128)} %reshape.115, f32[80,11,32,1]{0,2,1,3:T(8,128)S(1)} %bitcast.519), kind=kOutput, calls=%fused_computation.90 | convolution fusion | flops 27033600 | bytes 9134080 | tf_op jit(solution)/shard_map/ikab,bki->ai/dot_general | solution.py:104
  (591 shorter events, 226.5 us)
Async XLA Ops:
  86.6 14.1 %all-to-all-start = ((f32[80,16,2]{0,2,1:T(2,128)}), f32[80,16,2]{0,2,1:T(2,128)S(1)}, u32[]{:S(2)}, u32[]{:S(2)}) async-start(f32[80,16,2]{0,2,1:T(2,128)} %bitcast.63), calls=%async_computation | async-start | bytes 32768 | tf_op jit(solution)/shard_map/all_to_all | solution.py:108
  93.6 1.4 copy-start
  96.0 1.1 copy-start.1
  137.1 19.5 %all-to-all-start.1 = ((f32[80,2,16]{0,1,2:T(2,128)}), f32[80,2,16]{0,1,2:T(2,128)S(1)}, u32[]{:S(2)}, u32[]{:S(2)}) async-start(f32[80,2,16]{0,1,2:T(2,128)} %bitcast.71), calls=%async_computation.1 | async-start | bytes 32768 | tf_op jit(solution)/shard_map/all_to_all | solution.py:111
  157.2 11.4 %collective-permute-start = (f32[80,1,1,32]{0,3,2,1:T(8,128)S(1)}, f32[80,1,1,32]{0,3,2,1:T(8,128)S(1)}, u32[]{:S(2)}, u32[]{:S(2)}) collective-permute-start(f32[80,1,1,32]{0,3,2,1:T(8,128)S(1)} %bitcast.563), channel_id=1, source_target_pairs={{0,8},{8,16},{16,24},{24,32},{32,40},{40,48},{48,56},{56,64},{64,7... | collective-permute-start | bytes 30728 | tf_op jit(solution)/shard_map/ppermute | solution.py:20
  157.9 10.8 %collective-permute-start.1 = (f32[80,1,1,32]{0,3,2,1:T(8,128)S(1)}, f32[80,1,1,32]{0,3,2,1:T(8,128)S(1)}, u32[]{:S(2)}, u32[]{:S(2)}) collective-permute-start(f32[80,1,1,32]{0,3,2,1:T(8,128)S(1)} %bitcast.564), channel_id=1, source_target_pairs={{8,0},{16,8},{24,16},{32,24},{40,32},{48,40},{56,48},{64,56},{72,6... | collective-permute-start | bytes 30728 | tf_op jit(solution)/shard_map/ppermute | solution.py:21
  162.1 6.6 collective-permute-start.2
  166.2 5.1 collective-permute-start.3
  172.4 16.1 %copy-start.2 = (f32[80,32]{0,1:T(8,128)S(1)}, f32[80,32]{0,1:T(8,128)}, u32[]{:S(2)}) copy-start(f32[80,32]{0,1:T(8,128)} %param.23) | copy-start | bytes 30724
  339.5 8.6 all-to-all-start.2
  384.4 8.6 all-to-all-start.3
  393.7 10.3 %collective-permute-start.4 = (f32[80,1,1,32]{0,3,2,1:T(8,128)S(1)}, f32[80,1,1,32]{0,3,2,1:T(8,128)S(1)}, u32[]{:S(2)}, u32[]{:S(2)}) collective-permute-start(f32[80,1,1,32]{0,3,2,1:T(8,128)S(1)} %bitcast.567), channel_id=1, source_target_pairs={{0,8},{8,16},{16,24},{24,32},{32,40},{40,48},{48,56},{56,64},{64,7... | collective-permute-start | bytes 30728 | tf_op jit(solution)/shard_map/ppermute | solution.py:20
  394.7 9.4 %collective-permute-start.5 = (f32[80,1,1,32]{0,3,2,1:T(8,128)S(1)}, f32[80,1,1,32]{0,3,2,1:T(8,128)S(1)}, u32[]{:S(2)}, u32[]{:S(2)}) collective-permute-start(f32[80,1,1,32]{0,3,2,1:T(8,128)S(1)} %bitcast.568), channel_id=1, source_target_pairs={{8,0},{16,8},{24,16},{32,24},{40,32},{48,40},{56,48},{64,56},{72,6... | collective-permute-start | bytes 30728 | tf_op jit(solution)/shard_map/ppermute | solution.py:21
  398.6 5.5 collective-permute-start.6
  402.0 5.1 collective-permute-start.7
  573.6 8.6 all-to-all-start.4
  618.5 8.6 all-to-all-start.5
  627.8 10.4 %collective-permute-start.8 = (f32[80,1,1,32]{0,3,2,1:T(8,128)S(1)}, f32[80,1,1,32]{0,3,2,1:T(8,128)S(1)}, u32[]{:S(2)}, u32[]{:S(2)}) collective-permute-start(f32[80,1,1,32]{0,3,2,1:T(8,128)S(1)} %bitcast.571), channel_id=1, source_target_pairs={{0,8},{8,16},{16,24},{24,32},{32,40},{40,48},{48,56},{56,64},{64,7... | collective-permute-start | bytes 30728 | tf_op jit(solution)/shard_map/ppermute | solution.py:20
  628.9 9.3 %collective-permute-start.9 = (f32[80,1,1,32]{0,3,2,1:T(8,128)S(1)}, f32[80,1,1,32]{0,3,2,1:T(8,128)S(1)}, u32[]{:S(2)}, u32[]{:S(2)}) collective-permute-start(f32[80,1,1,32]{0,3,2,1:T(8,128)S(1)} %bitcast.572), channel_id=1, source_target_pairs={{8,0},{16,8},{24,16},{32,24},{40,32},{48,40},{56,48},{64,56},{72,6... | collective-permute-start | bytes 30728 | tf_op jit(solution)/shard_map/ppermute | solution.py:21
  632.7 5.5 collective-permute-start.10
  636.0 5.1 collective-permute-start.11
  821.6 8.6 all-to-all-start.6
  865.5 14.4 %copy-start.3 = (f32[80,32]{0,1:T(8,128)}, f32[80,32]{0,1:T(8,128)S(1)}, u32[]{:S(2)}) copy-start(f32[80,32]{0,1:T(8,128)S(1)} %scatter_custom_fusion.3) | copy-start | bytes 30724
  865.5 10.4 %collective-permute-start.12 = (f32[80,1,1,32]{0,3,2,1:T(8,128)S(1)}, f32[80,1,1,32]{0,3,2,1:T(8,128)S(1)}, u32[]{:S(2)}, u32[]{:S(2)}) collective-permute-start(f32[80,1,1,32]{0,3,2,1:T(8,128)S(1)} %bitcast.558), channel_id=1, source_target_pairs={{0,8},{8,16},{16,24},{24,32},{32,40},{40,48},{48,56},{56,64},{64,7... | collective-permute-start | bytes 30728 | tf_op jit(solution)/shard_map/ppermute | solution.py:20
  866.5 9.4 %collective-permute-start.13 = (f32[80,1,1,32]{0,3,2,1:T(8,128)S(1)}, f32[80,1,1,32]{0,3,2,1:T(8,128)S(1)}, u32[]{:S(2)}, u32[]{:S(2)}) collective-permute-start(f32[80,1,1,32]{0,3,2,1:T(8,128)S(1)} %bitcast.559), channel_id=1, source_target_pairs={{8,0},{16,8},{24,16},{32,24},{40,32},{48,40},{56,48},{64,56},{72,6... | collective-permute-start | bytes 30728 | tf_op jit(solution)/shard_map/ppermute | solution.py:21
  870.3 5.6 collective-permute-start.14
  873.7 5.1 collective-permute-start.15
where the time goes:
time: 908 us; the launch traced here: 897 us
  blocking collectives  528 us (58%)
  matrix products  169 us (19%)
  starting transfers between devices  71 us (8%)
  local copies, waits for them, and re-layouts  67.2 us (7%)
  waiting for transfers between devices  34.4 us (4%)
  between operations  14.2 us (2%)
  other arithmetic  12.1 us (1%)
    psum x3, blocking collectives, on_device(): square = lax.psum(jnp.sum(wvec * wvec), ('span', 'plane'))  220 us
    psum x3, blocking collectives, on_device(): hvals = lax.psum(local_proj, ('span', 'plane'))  219 us
    psum x1, blocking collectives, on_device(): beta = jnp.sqrt(lax.psum(jnp.sum(rhs * rhs), ('span', 'plane')) + 1e-06)  81.4 us
    dot_general x64, matrix products, forward(): cur = right - jnp.einsum('mab,bm->am', low, prev, precision=HIGH)  71.9 us
    dot_general x4, matrix products, apply_a(): return jnp.einsum('ikab,bki->ai', shaped_blocks, picked, precision=HIGH)  64.2 us
    dynamic_update_slice x64, local copies, waits for them, and re-layouts, line_solve(): _, yseq = lax.scan(forward, start, (rseq, lseq))  28.3 us
    ppermute x8, starting transfers between devices, with_halo(): after = lax.ppermute(first, axis, down)  24.5 us
  transfers between devices with their start and end apart: 23, of which 9 were waited for; matrix products, arithmetic and copies ran while one was open for 3% of the time, Pallas kernels for 0%

commit v1 on v0

v1 whole, which is shorter than its diff:
```python
import functools

import jax
import jax.numpy as jnp
from jax import lax
from jax.experimental import pallas as pl
from jax.experimental.pallas import tpu as pltpu
from jax.sharding import PartitionSpec as P

MESH = pl.DeviceIdType.MESH
F32 = jnp.float32
BF16 = jnp.bfloat16

B = 80
NBLK = 11
ITERS = 3
F = 32
W = 128
SEG = 640
NGRP = 10
PAIRS = [(i, j) for i in range(4) for j in range(i, 4)]


def iota(shape, axis):
    return lax.broadcasted_iota(jnp.int32, shape, axis)


def split(x):
    hi = x.astype(BF16)
    lo = (x - hi.astype(F32)).astype(BF16)
    return hi, lo


def bdot(a, b):
    return jnp.dot(a, b, preferred_element_type=F32)


def pad_lanes(x):
    return jnp.concatenate([x, jnp.zeros((x.shape[0], W - x.shape[1]), x.dtype)], axis=1)


def small_solve(factor, target):
    extent = len(target)
    forward_vals = []
    for row in range(extent):
        running = target[row]
        for inner in range(row):
            running = running - factor[row][inner] * forward_vals[inner]
        forward_vals.append(running / factor[row][row])
    backward_vals = [None] * extent
    for row in reversed(range(extent)):
        running = forward_vals[row]
        for inner in range(row + 1, extent):
            running = running - factor[inner][row] * backward_vals[inner]
        backward_vals[row] = running / factor[row][row]
    return backward_vals


def coefficients(gram):
    def inner(c, d):
        out = None
        for i in range(len(c)):
            for j in range(len(d)):
                term = c[i] * d[j] * gram[min(i, j), max(i, j)]
                out = term if out is None else out + term
        return out

    beta = jnp.sqrt(gram[0, 0] + 1e-6)
    zero = jnp.zeros_like(beta)
    basis = [[1.0 / beta]]
    h = [[zero] * ITERS for _ in range(ITERS + 1)]
    for step in range(ITERS):
        w = [zero] + basis[step]
        for i in range(step + 1):
            h[i][step] = inner(basis[i], w)
        for i in range(step + 1):
            for n, c in enumerate(basis[i]):
                w[n] = w[n] - h[i][step] * c
        h[step + 1][step] = jnp.sqrt(jnp.maximum(inner(w, w), 0.0) + 1e-6)
        basis.append([c / h[step + 1][step] for c in w])
    normal = [
        [sum(h[n][i] * h[n][j] for n in range(min(i, j) + 2)) for j in range(ITERS)]
        for i in range(ITERS)
    ]
    target = [beta * h[0][j] for j in range(ITERS)]
    factor = [[None] * ITERS for _ in range(ITERS)]
    for j in range(ITERS):
        diag = normal[j][j]
        for n in range(j):
            diag = diag - factor[j][n] * factor[j][n]
        factor[j][j] = jnp.sqrt(diag)
        for i in range(j + 1, ITERS):
            below = normal[i][j]
            for n in range(j):
                below = below - factor[i][n] * factor[j][n]
            factor[i][j] = below / factor[j][j]
    y = small_solve(factor, target)
    out = []
    for n in range(ITERS):
        out.append(sum(y[j] * basis[j][n] for j in range(n, ITERS)))
    return out


def kernel(
    rhs_ref, blocks_hbm, columns_ref, slot_ref, slot_smem, low_hbm, upp_hbm, piv_hbm,
    sol_ref, res_ref,
    blk, flat, tall, lm, pm, pum, kf, zf, rsend, rrecv, zsend, trecv, gid, onehot,
    thi, tlo, smat, square, ga, gb,
    load_sem, rsend_sem, rrecv_sem, zsend_sem, tplane_sem, tspan_sem, gsend_sem, grecv_sem,
    gas_sem, gar_sem, gbs_sem, gbr_sem,
):
    nspan, nplane = 32, 8
    s = lax.axis_index("span")
    p = lax.axis_index("plane")
    x, z = s // 8, s % 8
    s_next, s_prev = lax.rem(s + 1, nspan), lax.rem(s + nspan - 1, nspan)
    p_next, p_prev = lax.rem(p + 1, nplane), lax.rem(p + nplane - 1, nplane)

    def plane_at(i):
        return lax.rem(p + i, nplane)

    loads = []
    for n, src in enumerate((low_hbm, piv_hbm, upp_hbm)):
        loads.append(pltpu.make_async_copy(src, flat.at[n], load_sem.at[n]))
    for n in range(4):
        loads.append(
            pltpu.make_async_copy(
                blocks_hbm.at[pl.ds(8 * n, 8)], blk.at[pl.ds(8 * n, 8)], load_sem.at[3 + n]
            )
        )
    for load in loads:
        load.start()

    barrier = pltpu.get_barrier_semaphore()

    def span_partner(i):
        xx = lax.rem(x + i // 4, 4)
        zz = lax.rem(z + 2 * (i % 4), 8)
        return xx * 8 + zz

    def greet(device):
        pl.semaphore_signal(barrier, inc=1, device_id=device, device_id_type=MESH)

    for i in range(1, nplane):
        greet((s, plane_at(i)))
    for i in range(nplane):
        greet((s_next, plane_at(i)))
        greet((s_prev, plane_at(i)))
    for i in range(1, 16):
        greet((span_partner(i), p))

    k0 = pad_lanes(jnp.transpose(rhs_ref[...]))
    kf[0] = k0

    lane = iota((1, W), 1)
    def to_slots(it):
        for t in range(F):
            rsend[it, t // 4, pl.ds(t % 4, 1), :] = kf[it, pl.ds(slot_smem[0, t], 1), :]

    to_slots(0)
    mine = pad_lanes(slot_ref[...].astype(F32)) + ((s * nplane + p) * F).astype(F32)
    gid[0] = jnp.broadcast_to(mine, (8, W))

    pl.semaphore_wait(barrier, 7 + 16 + 15)

    def send_pieces(it):
        for i in range(1, nplane):
            to = plane_at(i)
            pltpu.make_async_remote_copy(
                src_ref=rsend.at[it, to], dst_ref=rrecv.at[it, p],
                send_sem=rsend_sem.at[it], recv_sem=rrecv_sem.at[it],
                device_id=(s, to), device_id_type=MESH,
            ).start()
        pltpu.make_async_copy(rsend.at[it, p], rrecv.at[it, p], rrecv_sem.at[it]).start()

    send_pieces(0)
    gid_copies = []
    for n, to in enumerate(((s, p_next), (s, p_prev), (s_next, p), (s_prev, p))):
        copy = pltpu.make_async_remote_copy(
            src_ref=gid.at[0], dst_ref=gid.at[n + 1],
            send_sem=gsend_sem.at[n], recv_sem=grecv_sem.at[n],
            device_id=to, device_id_type=MESH,
        )
        copy.start()
        gid_copies.append(copy)

    for n in range(3):
        loads[n].wait()

    def relayout(g, _):
        for n in range(3):
            chunk = flat[n, :, pl.ds(pl.multiple_of(g * SEG, W), SEG)]
            for a in range(8):
                tall[n, pl.ds(pl.multiple_of((g * 8 + a) * F, F), F), :] = pad_lanes(
                    chunk[:, a * B : (a + 1) * B]
                )
        return 0

    lax.fori_loop(0, NGRP, relayout, 0)

    zeros48 = jnp.zeros((W - B, W), F32)

    def flip(m):
        return jnp.transpose(jnp.concatenate([m, zeros48], axis=0))[:B]

    def prepare(c, _):
        for q in range(2):
            row = 2 * c + q

            def matrix(n):
                return tall[n, pl.ds(row, B, stride=F), :]

            low, piv, upp = matrix(0), matrix(1), matrix(2)
            ph, pl_ = split(piv[:, :B])
            uh, ul = split(upp)
            both = bdot(ph, uh) + (bdot(ph, ul) + bdot(pl_, uh))
            if q == 0:
                lm[row], pm[row], pum[row] = flip(low), piv, both
            else:
                lm[row], pm[row], pum[row] = low, flip(piv), flip(both)
        return 0

    lax.fori_loop(0, F // 2, prepare, 0)

    square[...] = jnp.zeros_like(square)
    for it in range(ITERS):
        zsend[it, 0] = jnp.zeros((4, W), F32)
        zsend[it, nplane + 1] = jnp.zeros((4, W), F32)
    thi[...] = jnp.zeros_like(thi)
    tlo[...] = jnp.zeros_like(tlo)
    smat[...] = (iota((SEG, W), 0) // B == iota((SEG, W), 1)).astype(F32).astype(BF16)

    for copy in gid_copies:
        copy.wait()
    below = jnp.where(p == 0, -1.0, gid[1])
    above = jnp.where(p == nplane - 1, -1.0, gid[2])
    rows = [below[0:1], gid[0][0:1], above[0:1], gid[3][0:1], gid[4][0:1]]
    stacked = jnp.concatenate(rows + [jnp.zeros((W - 5, W), F32)], axis=0)
    by_slot = jnp.transpose(stacked)[:F]
    n_at = iota((F, 2 * W), 1)
    blk_at = n_at // 4
    span_part = n_at >= 96
    dir_at = jnp.where(span_part, 3 + (blk_at - 24) // 8, blk_at % 3)
    slot_at = jnp.where(span_part, (n_at - 96) % F, (blk_at // 3) * 4 + n_at % 4)
    want = iota((F, 2 * W), 0) == slot_at
    numbers = jnp.zeros((F, 2 * W), F32)
    for d in range(5):
        numbers = numbers + jnp.where(want & (dir_at == d), by_slot[:, d : d + 1], 0.0)
    numbers = jnp.sum(numbers, axis=0, keepdims=True)
    numbers = jnp.where(iota((1, 2 * W), 1) < 160, numbers, -2.0)
    cols = jnp.transpose(
        jnp.concatenate(
            [pad_lanes(columns_ref[...].astype(F32)), jnp.zeros((W - NBLK, W), F32)], axis=0
        )
    )[:F]
    for g in range(4):
        for k in range(NBLK):
            onehot[pl.ds(g * 88 + k * 8, 8), :] = (
                cols[g * 8 : g * 8 + 8, k : k + 1] == numbers
            ).astype(F32)

    def one(it, _):
        pltpu.make_async_copy(rrecv.at[it], rrecv.at[it], rrecv_sem.at[it]).wait()
        for m in range(2):
            for c in range(8):
                square[pl.ds(m * 8 + c, 1), :] = rrecv[it, c, pl.ds(2 * m + 1, 1), :]
        odd = jnp.transpose(square[...])[:B]
        ys = [[], []]
        for j in range(16):
            for m in range(2):
                row = m * 16 + j
                if j == 0:
                    ys[m].append(rrecv[it, 0, pl.ds(2 * m, 1), :])
                elif j % 2:
                    idx = m * 8 + j // 2
                    base = jnp.where(lane == idx, odd, 0.0)
                    ys[m].append(
                        jnp.sum(base - lm[row] * ys[m][j - 1], axis=1, keepdims=True)
                    )
                else:
                    r = rrecv[it, j // 2, pl.ds(2 * m, 1), :]
                    ys[m].append(r - jnp.sum(lm[row] * ys[m][j - 1], axis=0, keepdims=True))
        zs = [None, None]
        even = jnp.zeros((B, W), F32)
        for j in reversed(range(16)):
            for m in range(2):
                row = m * 16 + j
                term = pm[row] * ys[m][j]
                if j < 15:
                    term = term - pum[row] * zs[m]
                zs[m] = jnp.sum(term, axis=j % 2 == 0 and 1 or 0, keepdims=True)
                if j % 2:
                    zsend[it, j // 2 + 1, pl.ds(2 * m + 1, 1), :] = zs[m]
                else:
                    even = jnp.where(lane == m * 8 + j // 2, zs[m], even)
        even = jnp.transpose(jnp.concatenate([even, zeros48], axis=0))
        for m in range(2):
            for c in range(8):
                zsend[it, c + 1, pl.ds(2 * m, 1), :] = even[m * 8 + c : m * 8 + c + 1]

        for i in range(nplane):
            to = plane_at(i)
            for n, there in enumerate((s_next, s_prev)):
                pltpu.make_async_remote_copy(
                    src_ref=zsend.at[it, to + 1], dst_ref=trecv.at[it, 24 + 8 * n + p],
                    send_sem=zsend_sem.at[it], recv_sem=tspan_sem.at[it],
                    device_id=(there, to), device_id_type=MESH,
                ).start()
        for i in range(1, nplane):
            to = plane_at(i)
            pltpu.make_async_remote_copy(
                src_ref=zsend.at[it, pl.ds(to, 3)], dst_ref=trecv.at[it, pl.ds(3 * p, 3)],
                send_sem=zsend_sem.at[it], recv_sem=tplane_sem.at[it],
                device_id=(s, to), device_id_type=MESH,
            ).start()
        pltpu.make_async_copy(
            zsend.at[it, pl.ds(p, 3)], trecv.at[it, pl.ds(3 * p, 3)], tplane_sem.at[it]
        ).start()

        part = trecv.at[it, pl.ds(0, 24)]
        pltpu.make_async_copy(part, part, tplane_sem.at[it]).wait()
        part = trecv.at[it, pl.ds(24, 16)]
        pltpu.make_async_copy(part, part, tspan_sem.at[it]).wait()

        got = trecv[it].reshape(160, W)[:, :B]
        wide = jnp.concatenate([got] * 8, axis=1)
        hi, lo = split(wide)
        thi[pl.ds(0, 160), :] = hi
        tlo[pl.ds(0, 160), :] = lo

        def faces(g, _):
            @pl.when(it == 0)
            def _():
                part = blk.at[pl.ds(pl.multiple_of(8 * g, 8), 8)]
                pltpu.make_async_copy(part, part, load_sem.at[3 + g]).wait()

            at = pl.ds(pl.multiple_of(8 * g, 8), 8)
            oh = onehot[pl.ds(pl.multiple_of(88 * g, 8), 88), :].astype(BF16)
            picked = bdot(oh, thi[...]) + bdot(oh, tlo[...])
            zf[it, at, :] = picked[:8, :W]
            sums = []
            for half in range(2):
                acc = None
                for k in range(NBLK):
                    term = blk[at, pl.ds(k * 6400 + half * 3200, 3200)] * jnp.concatenate(
                        [picked[8 * k : 8 * k + 8]] * 5, axis=1
                    )
                    acc = term if acc is None else acc + term
                sums += [acc[:, n * SEG : (n + 1) * SEG] for n in range(5)]
            hi, lo = split(jnp.concatenate(sums, axis=0))
            out = bdot(hi, smat[...]) + bdot(lo, smat[...])
            total = out[:8]
            for n in range(1, NGRP):
                total = total + pltpu.roll(out[8 * n : 8 * n + 8], 8 * n, 1)
            kf[it + 1, at, :] = total
            return 0

        lax.fori_loop(0, 4, faces, 0)

        @pl.when(it < ITERS - 1)
        def _():
            for t in range(F):
                rsend[it + 1, t // 4, pl.ds(t % 4, 1), :] = kf[
                    it + 1, pl.ds(slot_smem[0, t], 1), :
                ]
            send_pieces(it + 1)

        return 0

    lax.fori_loop(0, ITERS, one, 0)

    ks = [kf[i] for i in range(4)]
    place = iota((16, W), 0)
    tile = jnp.zeros((16, W), F32)
    for n, (i, j) in enumerate(PAIRS):
        prod = jnp.sum(jnp.sum(ks[i] * ks[j], axis=0, keepdims=True), axis=1, keepdims=True)
        tile = jnp.where(place == n, prod, tile)
    ga[0] = tile
    z_pair = z + 1 - 2 * lax.rem(z, 2)
    s_pair = x * 8 + z_pair
    for i in range(1, 16):
        to = (s, plane_at(i)) if i < 8 else (s_pair, plane_at(i - 8))
        pltpu.make_async_remote_copy(
            src_ref=ga.at[0], dst_ref=ga.at[i],
            send_sem=gas_sem.at[0], recv_sem=gar_sem.at[0],
            device_id=to, device_id_type=MESH,
        ).start()
    arrived = ga.at[pl.ds(1, 15)]
    pltpu.make_async_copy(arrived, arrived, gar_sem.at[0]).wait()
    gb[0] = jnp.sum(ga[...], axis=0)
    for i in range(1, 16):
        pltpu.make_async_remote_copy(
            src_ref=gb.at[0], dst_ref=gb.at[i],
            send_sem=gbs_sem.at[0], recv_sem=gbr_sem.at[0],
            device_id=(span_partner(i), p), device_id_type=MESH,
        ).start()
    arrived_b = gb.at[pl.ds(1, 15)]
    pltpu.make_async_copy(arrived_b, arrived_b, gbr_sem.at[0]).wait()
    whole = jnp.sum(gb[...], axis=0)
    gram = {pair: whole[n : n + 1] for n, pair in enumerate(PAIRS)}
    coef = coefficients(gram)
    solved = sum(coef[i] * zf[i] for i in range(ITERS))
    left = ks[0] - sum(coef[i] * ks[i + 1] for i in range(ITERS))
    sol_ref[...] = jnp.transpose(solved)[:B]
    res_ref[...] = jnp.transpose(left)[:B]

    pltpu.make_async_copy(arrived, arrived, gas_sem.at[0]).wait()
    pltpu.make_async_copy(arrived_b, arrived_b, gbs_sem.at[0]).wait()
    for it in range(ITERS):
        out = rsend.at[it, pl.ds(0, 7)]
        pltpu.make_async_copy(out, out, rsend_sem.at[it]).wait()
        out = trecv.at[it, pl.ds(0, 37)]
        pltpu.make_async_copy(out, out, zsend_sem.at[it]).wait()


def on_device(rhs, blocks, columns, line_slot, line_lower, line_upper, pivot_inv):
    vmem = pl.BlockSpec(memory_space=pltpu.VMEM)
    hbm = pl.BlockSpec(memory_space=pl.ANY)
    out = jax.ShapeDtypeStruct((B, F), F32)
    dma = pltpu.SemaphoreType.DMA
    return pl.pallas_call(
        kernel,
        out_shape=(out, out),
        in_specs=[vmem, hbm, vmem, vmem, pl.BlockSpec(memory_space=pltpu.SMEM), hbm, hbm, hbm],
        out_specs=(vmem, vmem),
        scratch_shapes=[
            pltpu.VMEM((F, NBLK * B * B), F32),
            pltpu.VMEM((3, F, B * B), F32),
            pltpu.VMEM((3, B * F, W), F32),
            pltpu.VMEM((F, B, W), F32),
            pltpu.VMEM((F, B, W), F32),
            pltpu.VMEM((F, B, W), F32),
            pltpu.VMEM((ITERS + 1, F, W), F32),
            pltpu.VMEM((ITERS, F, W), F32),
            pltpu.VMEM((ITERS, 8, 4, W), F32),
            pltpu.VMEM((ITERS, 8, 4, W), F32),
            pltpu.VMEM((ITERS, 10, 4, W), F32),
            pltpu.VMEM((ITERS, 40, 4, W), F32),
            pltpu.VMEM((5, 8, W), F32),
            pltpu.VMEM((4 * 88, 2 * W), F32),
            pltpu.VMEM((2 * W, SEG), BF16),
            pltpu.VMEM((2 * W, SEG), BF16),
            pltpu.VMEM((SEG, W), BF16),
            pltpu.VMEM((W, W), F32),
            pltpu.VMEM((16, 16, W), F32),
            pltpu.VMEM((16, 16, W), F32),
            dma((7,)),
            dma((ITERS,)),
            dma((ITERS,)),
            dma((ITERS,)),
            dma((ITERS,)),
            dma((ITERS,)),
            dma((4,)),
            dma((4,)),
            dma((1,)),
            dma((1,)),
            dma((1,)),
            dma((1,)),
        ],
        compiler_params=pltpu.CompilerParams(
            collective_id=0, has_side_effects=True, vmem_limit_bytes=48 * 1024 * 1024
        ),
    )(rhs, blocks, columns, line_slot, line_slot, line_lower, line_upper, pivot_inv)


def solution(mesh):
    return jax.shard_map(
        on_device,
        mesh=mesh,
        in_specs=(
            P(None, ("span", "plane")),
            P(("span", "plane"), None),
            P(None, ("span", "plane")),
            P(("span", "plane"), None),
            P(("span", "plane"), None),
            P(("span", "plane"), None),
            P(("span", "plane"), None),
        ),
        out_specs=(P(None, ("span", "plane")), P(None, ("span", "plane"))),
        check_vma=False,
    )
```

time: 908 us -> 74.9 us (0.08); the launches traced: 897 us -> 74.6 us
  blocking collectives: 528 us -> 0 us
  matrix products: 169 us -> 0 us
  starting transfers between devices: 71 us -> 0 us
  Pallas kernels: 0 us -> 67 us
  local copies, waits for them, and re-layouts: 67.2 us -> 6.94 us
  waiting for transfers between devices: 34.4 us -> 0 us
  between operations: 14.2 us -> 0.65 us
  other arithmetic: 12.1 us -> 0 us
    psum x7 -> x0, blocking collectives: 520 us -> none  [the longest x3 220 us: on_device(): square = lax.psum(jnp.sum(wvec * wvec), ('span', 'plane'))]
    dot_general x202 -> x0, matrix products: 169 us -> none  [the longest x64 71.9 us: forward(): cur = right - jnp.einsum('mab,bm->am', low, prev, precision=HIGH)]
    pallas_call x0 -> x1, Pallas kernels: none -> 67 us  [on_device(): pl.pallas_call(kernel, out_shape=(out, out), in_specs=[vmem, hbm, vmem, v...]
    ppermute x16 -> x0, starting transfers between devices: 42.4 us -> none  [the longest x8 24.5 us: with_halo(): after = lax.ppermute(first, axis, down)]
    all_to_all x7 -> x0, starting transfers between devices: 28.6 us -> none  [the longest x4 15.9 us: apply_m(): lax.all_to_all(pieces, 'plane', split_axis=1, concat_axis=2, tiled=True)]
    dynamic_update_slice x64 -> x0, local copies, waits for them, and re-layouts: 28.3 us -> none  [line_solve(): _, yseq = lax.scan(forward, start, (rseq, lseq))]
    all_to_all x7 -> x0, waiting for transfers between devices: 23.3 us -> none  [the longest x4 14 us: apply_m(): lax.all_to_all(pieces, 'plane', split_axis=1, concat_axis=2, tiled=True)]
    reshape x4 -> x0, local copies, waits for them, and re-layouts: 19.8 us -> none  [the longest x1 14.6 us: on_device(): shaped_blocks = blocks.reshape(nfaces, nblocks, width, width)]
  transfers between devices with their start and end apart: 23 -> 0, of which waited for: 9 -> 0; matrix products, arithmetic and copies ran while one was open for 3% -> 0% of each run, Pallas kernels for 0% -> 0%
where the time goes in v1:
time: 74.9 us; the launch traced here: 74.6 us
  Pallas kernels  67 us (89%)
  local copies, waits for them, and re-layouts  6.94 us (9%)
    pallas_call x1, Pallas kernels, on_device(): pl.pallas_call(kernel, out_shape=(out, out), in_specs=[vmem, hbm, vmem, v...  67 us
    unnamed x11, local copies, waits for them, and re-layouts  5.58 us

profile of v1, /device:TPU:1, one launch (start us, length us, event | category | flops | bytes accessed | tf_op | source)
XLA Modules:
  0.0 74.6 jit_solution(4473424585031234723)
XLA Ops:
  0.6 0.8 %copy.9.rhs_ref = f32[80,32]{1,0:T(8,128)S(1)} copy(f32[80,32]{0,1:T(8,128)} %param.7) | data formatting | bytes 20480 | tf_op args[0]
  1.4 0.0 copy-start
  1.4 1.1 %copy-done = f32[32,6400]{1,0:T(8,128)S(1)} copy-done((f32[32,6400]{1,0:T(8,128)S(1)}, f32[32,6400]{1,0:T(8,128)}, u32[]{:S(2)}) %copy-start) | copy-done | bytes 819224
  2.6 0.0 copy-start.1
  2.6 1.1 %copy-done.1 = f32[32,6400]{1,0:T(8,128)S(1)} copy-done((f32[32,6400]{1,0:T(8,128)S(1)}, f32[32,6400]{1,0:T(8,128)}, u32[]{:S(2)}) %copy-start.1) | copy-done | bytes 819224
  3.7 0.0 copy-start.2
  3.7 1.1 %copy-done.2 = f32[32,6400]{1,0:T(8,128)S(1)} copy-done((f32[32,6400]{1,0:T(8,128)S(1)}, f32[32,6400]{1,0:T(8,128)}, u32[]{:S(2)}) %copy-start.2) | copy-done | bytes 819224
  4.9 0.0 copy-start.3
  4.9 0.7 copy-done.3
  5.6 0.0 copy-start.4
  5.6 0.7 copy-done.4
  6.2 67.0 %shard_map.86 = (f32[80,32]{1,0:T(8,128)S(1)}, f32[80,32]{1,0:T(8,128)S(1)}) custom-call(f32[80,32]{1,0:T(8,128)S(1)} %copy.9.rhs_ref, f32[32,70400]{1,0:T(8,128)} %blocks_hbm.1, s32[11,32]{1,0:T(8,128)S(1)} %copy-done.3, s32[1,32]{1,0:T(1,128)S(1)} %copy-done.4, s32[1,32]{1,0:T(1,128)S(1)} %copy-done.4, f32[32,6400]{1,0:T(8,128)S(1)} %copy-done, ...), custom_call_target="tpu_custom_call" | custom-call | tf_op jit(solution)/shard_map/pallas_call | solution.py:421
  73.2 0.7 copy.10
  73.9 0.7 copy.11
Async XLA Ops:
  1.4 1.1 %copy-start = (f32[32,6400]{1,0:T(8,128)S(1)}, f32[32,6400]{1,0:T(8,128)}, u32[]{:S(2)}) copy-start(f32[32,6400]{1,0:T(8,128)} %low_hbm.1) | copy-start | bytes 2457604
  2.6 1.1 %copy-start.1 = (f32[32,6400]{1,0:T(8,128)S(1)}, f32[32,6400]{1,0:T(8,128)}, u32[]{:S(2)}) copy-start(f32[32,6400]{1,0:T(8,128)} %upp_hbm.1) | copy-start | bytes 2457604
  3.7 1.1 %copy-start.2 = (f32[32,6400]{1,0:T(8,128)S(1)}, f32[32,6400]{1,0:T(8,128)}, u32[]{:S(2)}) copy-start(f32[32,6400]{1,0:T(8,128)} %piv_hbm.1) | copy-start | bytes 2457604
  4.9 0.7 copy-start.3
  5.6 0.7 copy-start.4

commit v2 on v1

--- a/solution.py
+++ b/solution.py
@@ -18,6 +18,8 @@
 W = 128
 SEG = 640
 NGRP = 10
+EARLY = (0, 3, 4)
+LATE = (1, 2, 5, 6, 7, 8, 9, 10)
 PAIRS = [(i, j) for i in range(4) for j in range(i, 4)]
 
 
@@ -102,9 +104,9 @@
 
 
 def kernel(
-    rhs_ref, blocks_hbm, columns_ref, slot_ref, slot_smem, low_hbm, upp_hbm, piv_hbm,
+    rhs_hbm, blocks_hbm, columns_hbm, slot_hbm, low_hbm, upp_hbm, piv_hbm,
     sol_ref, res_ref,
-    blk, flat, tall, lm, pm, pum, kf, zf, rsend, rrecv, zsend, trecv, gid, onehot,
+    rhs_ref, columns_ref, slot_ref, slot_smem, blk, flat, tall, lm, pm, pum, kf, zf, rsend, rrecv, zsend, trecv, gid, early_hot, late_hot, xe, xl, acc,
     thi, tlo, smat, square, ga, gb,
     load_sem, rsend_sem, rrecv_sem, zsend_sem, tplane_sem, tspan_sem, gsend_sem, grecv_sem,
     gas_sem, gar_sem, gbs_sem, gbr_sem,
@@ -119,6 +121,15 @@
     def plane_at(i):
         return lax.rem(p + i, nplane)
 
+    small = []
+    for n, (src, dst) in enumerate(
+        (
+            (rhs_hbm, rhs_ref), (slot_hbm, slot_smem), (slot_hbm, slot_ref),
+            (columns_hbm, columns_ref),
+        )
+    ):
+        small.append(pltpu.make_async_copy(src, dst, load_sem.at[7 + n]))
+        small[-1].start()
     loads = []
     for n, src in enumerate((low_hbm, piv_hbm, upp_hbm)):
         loads.append(pltpu.make_async_copy(src, flat.at[n], load_sem.at[n]))
@@ -133,23 +144,23 @@
 
     barrier = pltpu.get_barrier_semaphore()
 
-    def span_partner(i):
-        xx = lax.rem(x + i // 4, 4)
-        zz = lax.rem(z + 2 * (i % 4), 8)
-        return xx * 8 + zz
+    def near(dx, dz):
+        return lax.rem(x + dx, 4) * 8 + lax.rem(z + dz, 8)
 
     def greet(device):
         pl.semaphore_signal(barrier, inc=1, device_id=device, device_id_type=MESH)
 
-    for i in range(1, nplane):
-        greet((s, plane_at(i)))
+    first = [(near(i // 8, 0), plane_at(i % 8)) for i in range(1, 32)]
+    second = [(near(0, i), p) for i in range(1, 8)]
     for i in range(nplane):
         greet((s_next, plane_at(i)))
         greet((s_prev, plane_at(i)))
-    for i in range(1, 16):
-        greet((span_partner(i), p))
-
-    k0 = pad_lanes(jnp.transpose(rhs_ref[...]))
+    for device in first + second:
+        greet(device)
+
+    for n in range(3):
+        small[n].wait()
+    k0 = pad_lanes(rhs_ref[...])
     kf[0] = k0
 
     lane = iota((1, W), 1)
@@ -160,8 +171,6 @@
     to_slots(0)
     mine = pad_lanes(slot_ref[...].astype(F32)) + ((s * nplane + p) * F).astype(F32)
     gid[0] = jnp.broadcast_to(mine, (8, W))
-
-    pl.semaphore_wait(barrier, 7 + 16 + 15)
 
     def send_pieces(it):
         for i in range(1, nplane):
@@ -173,6 +182,21 @@
             ).start()
         pltpu.make_async_copy(rsend.at[it, p], rrecv.at[it, p], rrecv_sem.at[it]).start()
 
+    for n in range(3):
+        loads[n].wait()
+
+    def relayout(g, _):
+        for n in range(3):
+            chunk = flat[n, :, pl.ds(pl.multiple_of(g * SEG, W), SEG)]
+            for a in range(8):
+                tall[n, pl.ds(pl.multiple_of((g * 8 + a) * F, F), F), :] = pad_lanes(
+                    chunk[:, a * B : (a + 1) * B]
+                )
+        return 0
+
+    lax.fori_loop(0, NGRP, relayout, 0)
+
+    pl.semaphore_wait(barrier, 16 + 31 + 7)
     send_pieces(0)
     gid_copies = []
     for n, to in enumerate(((s, p_next), (s, p_prev), (s_next, p), (s_prev, p))):
@@ -184,43 +208,29 @@
         copy.start()
         gid_copies.append(copy)
 
-    for n in range(3):
-        loads[n].wait()
-
-    def relayout(g, _):
-        for n in range(3):
-            chunk = flat[n, :, pl.ds(pl.multiple_of(g * SEG, W), SEG)]
-            for a in range(8):
-                tall[n, pl.ds(pl.multiple_of((g * 8 + a) * F, F), F), :] = pad_lanes(
-                    chunk[:, a * B : (a + 1) * B]
-                )
-        return 0
-
-    lax.fori_loop(0, NGRP, relayout, 0)
-
     zeros48 = jnp.zeros((W - B, W), F32)
 
     def flip(m):
         return jnp.transpose(jnp.concatenate([m, zeros48], axis=0))[:B]
 
     def prepare(c, _):
-        for q in range(2):
-            row = 2 * c + q
-
-            def matrix(n):
-                return tall[n, pl.ds(row, B, stride=F), :]
+        for n in range(8):
+            row = 8 * c + n
+
+            def matrix(which):
+                return tall[which, pl.ds(row, B, stride=F), :]
 
             low, piv, upp = matrix(0), matrix(1), matrix(2)
             ph, pl_ = split(piv[:, :B])
             uh, ul = split(upp)
             both = bdot(ph, uh) + (bdot(ph, ul) + bdot(pl_, uh))
-            if q == 0:
+            if n % 2 == 0:
                 lm[row], pm[row], pum[row] = flip(low), piv, both
             else:
                 lm[row], pm[row], pum[row] = low, flip(piv), flip(both)
         return 0
 
-    lax.fori_loop(0, F // 2, prepare, 0)
+    lax.fori_loop(0, F // 8, prepare, 0)
 
     square[...] = jnp.zeros_like(square)
     for it in range(ITERS):
@@ -248,16 +258,34 @@
         numbers = numbers + jnp.where(want & (dir_at == d), by_slot[:, d : d + 1], 0.0)
     numbers = jnp.sum(numbers, axis=0, keepdims=True)
     numbers = jnp.where(iota((1, 2 * W), 1) < 160, numbers, -2.0)
+    small[3].wait()
     cols = jnp.transpose(
         jnp.concatenate(
             [pad_lanes(columns_ref[...].astype(F32)), jnp.zeros((W - NBLK, W), F32)], axis=0
         )
     )[:F]
-    for g in range(4):
-        for k in range(NBLK):
-            onehot[pl.ds(g * 88 + k * 8, 8), :] = (
-                cols[g * 8 : g * 8 + 8, k : k + 1] == numbers
-            ).astype(F32)
+    for n, k in enumerate(EARLY):
+        early_hot[pl.ds(n * F, F), :] = (cols[:, k : k + 1] == numbers[:, :W]).astype(BF16)
+    for n, k in enumerate(LATE):
+        late_hot[pl.ds(n * F, F), :] = (cols[:, k : k + 1] == numbers).astype(BF16)
+    for n in range(4):
+        loads[3 + n].wait()
+
+    def widen(it, start, count):
+        got = trecv[it, pl.ds(start, count)].reshape(4 * count, W)[:, :B]
+        hi, lo = split(jnp.concatenate([got] * 8, axis=1))
+        thi[pl.ds(4 * start, 4 * count), :] = hi
+        tlo[pl.ds(4 * start, 4 * count), :] = lo
+
+    def weigh(g, half, which, picked, total):
+        at = pl.ds(pl.multiple_of(8 * g, 8), 8)
+        for n, k in enumerate(which):
+            wide = picked[pl.ds(pl.multiple_of(n * F + 8 * g, 8), 8), :]
+            term = blk[at, pl.ds(k * 6400 + half * 3200, 3200)] * jnp.concatenate(
+                [wide] * 5, axis=1
+            )
+            total = term if total is None else total + term
+        return total
 
     def one(it, _):
         pltpu.make_async_copy(rrecv.at[it], rrecv.at[it], rrecv_sem.at[it]).wait()
@@ -319,34 +347,31 @@
 
         part = trecv.at[it, pl.ds(0, 24)]
         pltpu.make_async_copy(part, part, tplane_sem.at[it]).wait()
+        widen(it, 0, 24)
+        hot = early_hot[...]
+        xe[...] = bdot(hot, thi[pl.ds(0, W), :]) + bdot(hot, tlo[pl.ds(0, W), :])
+        zf[it] = xe[pl.ds(0, F), pl.ds(0, W)]
+
+        def early(g, _):
+            at = pl.ds(pl.multiple_of(8 * g, 8), 8)
+            for half in range(2):
+                acc[at, pl.ds(half * 3200, 3200)] = weigh(g, half, EARLY, xe, None)
+            return 0
+
+        lax.fori_loop(0, 4, early, 0)
+
         part = trecv.at[it, pl.ds(24, 16)]
         pltpu.make_async_copy(part, part, tspan_sem.at[it]).wait()
-
-        got = trecv[it].reshape(160, W)[:, :B]
-        wide = jnp.concatenate([got] * 8, axis=1)
-        hi, lo = split(wide)
-        thi[pl.ds(0, 160), :] = hi
-        tlo[pl.ds(0, 160), :] = lo
-
-        def faces(g, _):
-            @pl.when(it == 0)
-            def _():
-                part = blk.at[pl.ds(pl.multiple_of(8 * g, 8), 8)]
-                pltpu.make_async_copy(part, part, load_sem.at[3 + g]).wait()
-
+        widen(it, 24, 16)
+        hot = late_hot[...]
+        xl[...] = bdot(hot, thi[...]) + bdot(hot, tlo[...])
+
+        def late(g, _):
             at = pl.ds(pl.multiple_of(8 * g, 8), 8)
-            oh = onehot[pl.ds(pl.multiple_of(88 * g, 8), 88), :].astype(BF16)
-            picked = bdot(oh, thi[...]) + bdot(oh, tlo[...])
-            zf[it, at, :] = picked[:8, :W]
             sums = []
             for half in range(2):
-                acc = None
-                for k in range(NBLK):
-                    term = blk[at, pl.ds(k * 6400 + half * 3200, 3200)] * jnp.concatenate(
-                        [picked[8 * k : 8 * k + 8]] * 5, axis=1
-                    )
-                    acc = term if acc is None else acc + term
-                sums += [acc[:, n * SEG : (n + 1) * SEG] for n in range(5)]
+                total = weigh(g, half, LATE, xl, acc[at, pl.ds(half * 3200, 3200)])
+                sums += [total[:, n * SEG : (n + 1) * SEG] for n in range(5)]
             hi, lo = split(jnp.concatenate(sums, axis=0))
             out = bdot(hi, smat[...]) + bdot(lo, smat[...])
             total = out[:8]
@@ -355,7 +380,7 @@
             kf[it + 1, at, :] = total
             return 0
 
-        lax.fori_loop(0, 4, faces, 0)
+        lax.fori_loop(0, 4, late, 0)
 
         @pl.when(it < ITERS - 1)
         def _():
@@ -370,39 +395,40 @@
     lax.fori_loop(0, ITERS, one, 0)
 
     ks = [kf[i] for i in range(4)]
-    place = iota((16, W), 0)
-    tile = jnp.zeros((16, W), F32)
-    for n, (i, j) in enumerate(PAIRS):
-        prod = jnp.sum(jnp.sum(ks[i] * ks[j], axis=0, keepdims=True), axis=1, keepdims=True)
-        tile = jnp.where(place == n, prod, tile)
-    ga[0] = tile
-    z_pair = z + 1 - 2 * lax.rem(z, 2)
-    s_pair = x * 8 + z_pair
-    for i in range(1, 16):
-        to = (s, plane_at(i)) if i < 8 else (s_pair, plane_at(i - 8))
+    tile = jnp.concatenate(
+        [jnp.sum(ks[i] * ks[j], axis=0, keepdims=True) for i, j in PAIRS]
+        + [jnp.zeros((6, W), F32)],
+        axis=0,
+    )
+    tile = jnp.sum(tile, axis=1, keepdims=True)
+    tile = jnp.where(iota((16, W), 0) == iota((16, W), 1), tile, 0.0)
+    ga[0] = jnp.sum(tile, axis=0, keepdims=True)
+    for i, to in enumerate(first):
         pltpu.make_async_remote_copy(
-            src_ref=ga.at[0], dst_ref=ga.at[i],
+            src_ref=ga.at[0], dst_ref=ga.at[i + 1],
             send_sem=gas_sem.at[0], recv_sem=gar_sem.at[0],
             device_id=to, device_id_type=MESH,
         ).start()
-    arrived = ga.at[pl.ds(1, 15)]
+    arrived = ga.at[pl.ds(1, 31)]
     pltpu.make_async_copy(arrived, arrived, gar_sem.at[0]).wait()
     gb[0] = jnp.sum(ga[...], axis=0)
-    for i in range(1, 16):
+    for i, to in enumerate(second):
         pltpu.make_async_remote_copy(
-            src_ref=gb.at[0], dst_ref=gb.at[i],
+            src_ref=gb.at[0], dst_ref=gb.at[i + 1],
             send_sem=gbs_sem.at[0], recv_sem=gbr_sem.at[0],
-            device_id=(span_partner(i), p), device_id_type=MESH,
+            device_id=to, device_id_type=MESH,
         ).start()
-    arrived_b = gb.at[pl.ds(1, 15)]
+    arrived_b = gb.at[pl.ds(1, 7)]
     pltpu.make_async_copy(arrived_b, arrived_b, gbr_sem.at[0]).wait()
     whole = jnp.sum(gb[...], axis=0)
-    gram = {pair: whole[n : n + 1] for n, pair in enumerate(PAIRS)}
+    gram = {
+        pair: jnp.broadcast_to(whole[:, n : n + 1], (1, W)) for n, pair in enumerate(PAIRS)
+    }
     coef = coefficients(gram)
     solved = sum(coef[i] * zf[i] for i in range(ITERS))
     left = ks[0] - sum(coef[i] * ks[i + 1] for i in range(ITERS))
-    sol_ref[...] = jnp.transpose(solved)[:B]
-    res_ref[...] = jnp.transpose(left)[:B]
+    sol_ref[...] = solved[:, :B]
+    res_ref[...] = left[:, :B]
 
     pltpu.make_async_copy(arrived, arrived, gas_sem.at[0]).wait()
     pltpu.make_async_copy(arrived_b, arrived_b, gbs_sem.at[0]).wait()
@@ -416,14 +442,18 @@
 def on_device(rhs, blocks, columns, line_slot, line_lower, line_upper, pivot_inv):
     vmem = pl.BlockSpec(memory_space=pltpu.VMEM)
     hbm = pl.BlockSpec(memory_space=pl.ANY)
-    out = jax.ShapeDtypeStruct((B, F), F32)
+    out = jax.ShapeDtypeStruct((F, B), F32)
     dma = pltpu.SemaphoreType.DMA
-    return pl.pallas_call(
+    solved, left = pl.pallas_call(
         kernel,
         out_shape=(out, out),
-        in_specs=[vmem, hbm, vmem, vmem, pl.BlockSpec(memory_space=pltpu.SMEM), hbm, hbm, hbm],
+        in_specs=[hbm] * 7,
         out_specs=(vmem, vmem),
         scratch_shapes=[
+            pltpu.VMEM((F, B), F32),
+            pltpu.VMEM((NBLK, F), jnp.int32),
+            pltpu.VMEM((1, F), jnp.int32),
+            pltpu.SMEM((1, F), jnp.int32),
             pltpu.VMEM((F, NBLK * B * B), F32),
             pltpu.VMEM((3, F, B * B), F32),
             pltpu.VMEM((3, B * F, W), F32),
@@ -437,14 +467,18 @@
             pltpu.VMEM((ITERS, 10, 4, W), F32),
             pltpu.VMEM((ITERS, 40, 4, W), F32),
             pltpu.VMEM((5, 8, W), F32),
-            pltpu.VMEM((4 * 88, 2 * W), F32),
+            pltpu.VMEM((3 * F, W), BF16),
+            pltpu.VMEM((8 * F, 2 * W), BF16),
+            pltpu.VMEM((3 * F, SEG), F32),
+            pltpu.VMEM((8 * F, SEG), F32),
+            pltpu.VMEM((F, B * B), F32),
             pltpu.VMEM((2 * W, SEG), BF16),
             pltpu.VMEM((2 * W, SEG), BF16),
             pltpu.VMEM((SEG, W), BF16),
             pltpu.VMEM((W, W), F32),
-            pltpu.VMEM((16, 16, W), F32),
-            pltpu.VMEM((16, 16, W), F32),
-            dma((7,)),
+            pltpu.VMEM((32, 1, W), F32),
+            pltpu.VMEM((8, 1, W), F32),
+            dma((11,)),
             dma((ITERS,)),
             dma((ITERS,)),
             dma((ITERS,)),
@@ -458,9 +492,10 @@
             dma((1,)),
         ],
         compiler_params=pltpu.CompilerParams(
-            collective_id=0, has_side_effects=True, vmem_limit_bytes=48 * 1024 * 1024
+            collective_id=0, has_side_effects=True, vmem_limit_bytes=60 * 1024 * 1024
         ),
-    )(rhs, blocks, columns, line_slot, line_slot, line_lower, line_upper, pivot_inv)
+    )(rhs.T, blocks, columns, line_slot, line_lower, line_upper, pivot_inv)
+    return solved.T, left.T
 
 
 def solution(mesh):

time: 74.9 us -> 62.4 us (0.83)
  Pallas kernels: 67 us -> 58.7 us
  local copies, waits for them, and re-layouts: 6.94 us -> 2.65 us
    pallas_call x1, Pallas kernels: 67 us -> 58.7 us  [on_device(): pl.pallas_call(kernel, out_shape=(out, out), in_specs=[hbm] * 7, out_spec...]
    unnamed x11 -> x2, local copies, waits for them, and re-layouts: 5.58 us -> 2.65 us
    pallas_call x2 -> x0, local copies, waits for them, and re-layouts: 1.36 us -> none  [on_device(): pl.pallas_call(kernel, out_shape=(out, out), in_specs=[vmem, hbm, vmem, v...]
where the time goes in v2:
time: 62.4 us; the launch traced here: 62 us
  Pallas kernels  58.7 us (94%)
  local copies, waits for them, and re-layouts  2.65 us (4%)
  between operations  0.64 us (1%)
    pallas_call x1, Pallas kernels, on_device(): pl.pallas_call(kernel, out_shape=(out, out), in_specs=[hbm] * 7, out_spec...  58.7 us
    unnamed x2, local copies, waits for them, and re-layouts  2.65 us

profile of v2, /device:TPU:1, one launch (start us, length us, event | category | flops | bytes accessed | tf_op | source)
XLA Modules:
  0.0 62.0 jit_solution(8651707331122668983)
XLA Ops:
  0.6 58.7 %shard_map.86 = (f32[32,80]{1,0:T(8,128)}, f32[32,80]{1,0:T(8,128)}) custom-call(f32[32,80]{1,0:T(8,128)} %bitcast.3, f32[32,70400]{1,0:T(8,128)} %blocks_hbm.1, s32[11,32]{1,0:T(8,128)} %columns_hbm.1, s32[1,32]{1,0:T(1,128)} %slot_hbm.1, f32[32,6400]{1,0:T(8,128)} %low_hbm.1, f32[32,6400]{1,0:T(8,128)} %upp_hbm.1, f32[32,6400]{1,0:T(8,128)} %piv_hbm.1), custom_call_target="tpu_custom_call" | custom-call | tf_op jit(solution)/shard_map/pallas_call | solution.py:447
  59.4 1.3 %copy.11 = f32[80,32]{0,1:T(8,128)} copy(f32[80,32]{0,1:T(8,128)} %bitcast.5) | data formatting | bytes 20480
  60.7 1.3 %copy.12 = f32[80,32]{0,1:T(8,128)} copy(f32[80,32]{0,1:T(8,128)} %bitcast.4) | data formatting | bytes 20480

commit v3 on v2

--- a/solution.py
+++ b/solution.py
@@ -105,8 +105,8 @@
 
 def kernel(
     rhs_hbm, blocks_hbm, columns_hbm, slot_hbm, low_hbm, upp_hbm, piv_hbm,
-    sol_ref, res_ref,
-    rhs_ref, columns_ref, slot_ref, slot_smem, blk, flat, tall, lm, pm, pum, kf, zf, rsend, rrecv, zsend, trecv, gid, early_hot, late_hot, xe, xl, acc,
+    both_ref,
+    rhs_ref, columns_ref, slot_ref, slot_smem, blk, flat, tall, lm, pm, pum, kf, zf, rsend, rrecv, zsend, trecv, gid, early_hot, late_hot, xe, xl, acc, acc2, sfull,
     thi, tlo, smat, square, ga, gb,
     load_sem, rsend_sem, rrecv_sem, zsend_sem, tplane_sem, tspan_sem, gsend_sem, grecv_sem,
     gas_sem, gar_sem, gbs_sem, gbr_sem,
@@ -238,7 +238,13 @@
         zsend[it, nplane + 1] = jnp.zeros((4, W), F32)
     thi[...] = jnp.zeros_like(thi)
     tlo[...] = jnp.zeros_like(tlo)
-    smat[...] = (iota((SEG, W), 0) // B == iota((SEG, W), 1)).astype(F32).astype(BF16)
+    def ones(n, _):
+        at = pl.ds(pl.multiple_of(n * SEG, SEG), SEG)
+        match = (n * SEG + iota((SEG, W), 0)) // B == iota((SEG, W), 1)
+        sfull[at, :] = match.astype(F32).astype(BF16)
+        return 0
+
+    lax.fori_loop(0, NGRP, ones, 0)
 
     for copy in gid_copies:
         copy.wait()
@@ -277,12 +283,11 @@
         thi[pl.ds(4 * start, 4 * count), :] = hi
         tlo[pl.ds(4 * start, 4 * count), :] = lo
 
-    def weigh(g, half, which, picked, total):
-        at = pl.ds(pl.multiple_of(8 * g, 8), 8)
+    def weigh(row, half, which, picked, total):
+        at = pl.ds(row, 8)
         for n, k in enumerate(which):
-            wide = picked[pl.ds(pl.multiple_of(n * F + 8 * g, 8), 8), :]
             term = blk[at, pl.ds(k * 6400 + half * 3200, 3200)] * jnp.concatenate(
-                [wide] * 5, axis=1
+                [picked[pl.ds(n * F + row, 8), :]] * 5, axis=1
             )
             total = term if total is None else total + term
         return total
@@ -352,13 +357,9 @@
         xe[...] = bdot(hot, thi[pl.ds(0, W), :]) + bdot(hot, tlo[pl.ds(0, W), :])
         zf[it] = xe[pl.ds(0, F), pl.ds(0, W)]
 
-        def early(g, _):
-            at = pl.ds(pl.multiple_of(8 * g, 8), 8)
+        for row in range(0, F, 8):
             for half in range(2):
-                acc[at, pl.ds(half * 3200, 3200)] = weigh(g, half, EARLY, xe, None)
-            return 0
-
-        lax.fori_loop(0, 4, early, 0)
+                acc[pl.ds(row, 8), pl.ds(half * 3200, 3200)] = weigh(row, half, EARLY, xe, None)
 
         part = trecv.at[it, pl.ds(24, 16)]
         pltpu.make_async_copy(part, part, tspan_sem.at[it]).wait()
@@ -366,21 +367,20 @@
         hot = late_hot[...]
         xl[...] = bdot(hot, thi[...]) + bdot(hot, tlo[...])
 
-        def late(g, _):
-            at = pl.ds(pl.multiple_of(8 * g, 8), 8)
-            sums = []
-            for half in range(2):
-                total = weigh(g, half, LATE, xl, acc[at, pl.ds(half * 3200, 3200)])
-                sums += [total[:, n * SEG : (n + 1) * SEG] for n in range(5)]
-            hi, lo = split(jnp.concatenate(sums, axis=0))
-            out = bdot(hi, smat[...]) + bdot(lo, smat[...])
-            total = out[:8]
-            for n in range(1, NGRP):
-                total = total + pltpu.roll(out[8 * n : 8 * n + 8], 8 * n, 1)
-            kf[it + 1, at, :] = total
-            return 0
-
-        lax.fori_loop(0, 4, late, 0)
+        out = None
+        for half in range(2):
+            lanes = pl.ds(half * 3200, 3200)
+            for row in range(0, F, 16):
+                total = jnp.concatenate(
+                    [weigh(n, half, LATE, xl, acc[pl.ds(n, 8), lanes]) for n in (row, row + 8)],
+                    axis=0,
+                )
+                hi, lo = split(total)
+                acc2[pl.ds(row, 16), lanes] = hi
+                acc2[pl.ds(F + row, 16), lanes] = lo
+            part = bdot(acc2[:, lanes], sfull[lanes, :])
+            out = part if out is None else out + part
+        kf[it + 1] = out[:F] + out[F:]
 
         @pl.when(it < ITERS - 1)
         def _():
@@ -427,8 +427,8 @@
     coef = coefficients(gram)
     solved = sum(coef[i] * zf[i] for i in range(ITERS))
     left = ks[0] - sum(coef[i] * ks[i + 1] for i in range(ITERS))
-    sol_ref[...] = solved[:, :B]
-    res_ref[...] = left[:, :B]
+    both_ref[0] = solved[:, :B]
+    both_ref[1] = left[:, :B]
 
     pltpu.make_async_copy(arrived, arrived, gas_sem.at[0]).wait()
     pltpu.make_async_copy(arrived_b, arrived_b, gbs_sem.at[0]).wait()
@@ -444,11 +444,11 @@
     hbm = pl.BlockSpec(memory_space=pl.ANY)
     out = jax.ShapeDtypeStruct((F, B), F32)
     dma = pltpu.SemaphoreType.DMA
-    solved, left = pl.pallas_call(
+    both = pl.pallas_call(
         kernel,
-        out_shape=(out, out),
+        out_shape=jax.ShapeDtypeStruct((2, F, B), F32),
         in_specs=[hbm] * 7,
-        out_specs=(vmem, vmem),
+        out_specs=vmem,
         scratch_shapes=[
             pltpu.VMEM((F, B), F32),
             pltpu.VMEM((NBLK, F), jnp.int32),
@@ -472,6 +472,8 @@
             pltpu.VMEM((3 * F, SEG), F32),
             pltpu.VMEM((8 * F, SEG), F32),
             pltpu.VMEM((F, B * B), F32),
+            pltpu.VMEM((2 * F, B * B), BF16),
+            pltpu.VMEM((B * B, W), BF16),
             pltpu.VMEM((2 * W, SEG), BF16),
             pltpu.VMEM((2 * W, SEG), BF16),
             pltpu.VMEM((SEG, W), BF16),
@@ -495,7 +497,7 @@
             collective_id=0, has_side_effects=True, vmem_limit_bytes=60 * 1024 * 1024
         ),
     )(rhs.T, blocks, columns, line_slot, line_lower, line_upper, pivot_inv)
-    return solved.T, left.T
+    return both[0].T, both[1].T
 
 
 def solution(mesh):

time: 62.4 us -> 61.5 us (0.986)
  local copies, waits for them, and re-layouts: 2.65 us -> 1.35 us
    unnamed x2 -> x0, local copies, waits for them, and re-layouts: 2.65 us -> none
    transpose x0 -> x1, local copies, waits for them, and re-layouts: none -> 1.35 us  [on_device(): return (both[0].T, both[1].T)]
where the time goes in v3:
time: 61.5 us; the launch traced here: 61.2 us
  Pallas kernels  59.2 us (96%)
  local copies, waits for them, and re-layouts  1.35 us (2%)
  between operations  0.64 us (1%)
    pallas_call x1, Pallas kernels, on_device(): pl.pallas_call(kernel, out_shape=jax.ShapeDtypeStruct((2, F, B), F32), in...  59.2 us
    transpose x1, local copies, waits for them, and re-layouts, on_device(): return (both[0].T, both[1].T)  1.35 us

profile of v3, /device:TPU:1, one launch (start us, length us, event | category | flops | bytes accessed | tf_op | source)
XLA Modules:
  0.0 61.2 jit_solution(10733012303623437396)
XLA Ops:
  0.6 59.2 %shard_map.86 = f32[2,32,80]{2,1,0:T(8,128)} custom-call(f32[32,80]{1,0:T(8,128)} %bitcast.9, f32[32,70400]{1,0:T(8,128)} %blocks_hbm.1, s32[11,32]{1,0:T(8,128)} %columns_hbm.1, s32[1,32]{1,0:T(1,128)} %slot_hbm.1, f32[32,6400]{1,0:T(8,128)} %low_hbm.1, f32[32,6400]{1,0:T(8,128)} %upp_hbm.1, f32[32,6400]{1,0:T(8,128)} %piv_hbm.1), custom_call_target="tpu_custom_call" | custom-call | tf_op jit(solution)/shard_map/pallas_call | solution.py:447
  59.8 1.3 %slice_bitcast_fusion = (f32[80,32]{0,1:T(8,128)}, f32[80,32]{0,1:T(8,128)}) fusion(f32[2,32,80]{2,1,0:T(8,128)} %shard_map.86), kind=kLoop, calls=%fused_computation | loop fusion | bytes 40960 | tf_op jit(solution)/shard_map/transpose | solution.py:500

commit v4 on v3

--- a/solution.py
+++ b/solution.py
@@ -238,44 +238,48 @@
         zsend[it, nplane + 1] = jnp.zeros((4, W), F32)
     thi[...] = jnp.zeros_like(thi)
     tlo[...] = jnp.zeros_like(tlo)
-    def ones(n, _):
-        at = pl.ds(pl.multiple_of(n * SEG, SEG), SEG)
-        match = (n * SEG + iota((SEG, W), 0)) // B == iota((SEG, W), 1)
-        sfull[at, :] = match.astype(F32).astype(BF16)
-        return 0
-
-    lax.fori_loop(0, NGRP, ones, 0)
-
-    for copy in gid_copies:
-        copy.wait()
-    below = jnp.where(p == 0, -1.0, gid[1])
-    above = jnp.where(p == nplane - 1, -1.0, gid[2])
-    rows = [below[0:1], gid[0][0:1], above[0:1], gid[3][0:1], gid[4][0:1]]
-    stacked = jnp.concatenate(rows + [jnp.zeros((W - 5, W), F32)], axis=0)
-    by_slot = jnp.transpose(stacked)[:F]
-    n_at = iota((F, 2 * W), 1)
-    blk_at = n_at // 4
-    span_part = n_at >= 96
-    dir_at = jnp.where(span_part, 3 + (blk_at - 24) // 8, blk_at % 3)
-    slot_at = jnp.where(span_part, (n_at - 96) % F, (blk_at // 3) * 4 + n_at % 4)
-    want = iota((F, 2 * W), 0) == slot_at
-    numbers = jnp.zeros((F, 2 * W), F32)
-    for d in range(5):
-        numbers = numbers + jnp.where(want & (dir_at == d), by_slot[:, d : d + 1], 0.0)
-    numbers = jnp.sum(numbers, axis=0, keepdims=True)
-    numbers = jnp.where(iota((1, 2 * W), 1) < 160, numbers, -2.0)
-    small[3].wait()
-    cols = jnp.transpose(
-        jnp.concatenate(
-            [pad_lanes(columns_ref[...].astype(F32)), jnp.zeros((W - NBLK, W), F32)], axis=0
-        )
-    )[:F]
-    for n, k in enumerate(EARLY):
-        early_hot[pl.ds(n * F, F), :] = (cols[:, k : k + 1] == numbers[:, :W]).astype(BF16)
-    for n, k in enumerate(LATE):
-        late_hot[pl.ds(n * F, F), :] = (cols[:, k : k + 1] == numbers).astype(BF16)
-    for n in range(4):
-        loads[3 + n].wait()
+
+    def set_up():
+        for copy in gid_copies:
+            copy.wait()
+        below = jnp.where(p == 0, -1.0, gid[1])
+        above = jnp.where(p == nplane - 1, -1.0, gid[2])
+        rows = [below[0:1], gid[0][0:1], above[0:1], gid[3][0:1], gid[4][0:1]]
+        stacked = jnp.concatenate(rows + [jnp.zeros((W - 5, W), F32)], axis=0)
+        by_slot = jnp.transpose(stacked)[:F]
+        n_at = iota((1, 2 * W), 1)
+        blk_at = n_at // 4
+        span_part = n_at >= 96
+        dir_at = jnp.where(span_part, 3 + (blk_at - 24) // 8, blk_at % 3)
+        slot_at = jnp.where(span_part, (n_at - 96) % F, (blk_at // 3) * 4 + n_at % 4)
+        want = iota((F, 2 * W), 0) == slot_at
+        numbers = jnp.zeros((F, 2 * W), F32)
+        for d in range(5):
+            numbers = numbers + jnp.where(want & (dir_at == d), by_slot[:, d : d + 1], 0.0)
+        numbers = jnp.sum(numbers, axis=0, keepdims=True)
+        numbers = jnp.where(iota((1, 2 * W), 1) < 160, numbers, -2.0)
+        small[3].wait()
+        cols = jnp.transpose(
+            jnp.concatenate(
+                [pad_lanes(columns_ref[...].astype(F32)), jnp.zeros((W - NBLK, W), F32)], axis=0
+            )
+        )[:F]
+        for n, k in enumerate(EARLY):
+            early_hot[pl.ds(n * F, F), :] = (cols[:, k : k + 1] == numbers[:, :W]).astype(BF16)
+        for n, k in enumerate(LATE):
+            late_hot[pl.ds(n * F, F), :] = (cols[:, k : k + 1] == numbers).astype(BF16)
+        for n in range(4):
+            loads[3 + n].wait()
+        start = iota((SEG, W), 1) * B - iota((SEG, W), 0)
+
+        def ones(n, _):
+            ahead = start - n * SEG
+            sfull[pl.ds(pl.multiple_of(n * SEG, SEG), SEG), :] = jnp.where(
+                (ahead <= 0) & (ahead > -B), 1.0, 0.0
+            ).astype(BF16)
+            return 0
+
+        lax.fori_loop(0, NGRP, ones, 0)
 
     def widen(it, start, count):
         got = trecv[it, pl.ds(start, count)].reshape(4 * count, W)[:, :B]
@@ -349,6 +353,10 @@
         pltpu.make_async_copy(
             zsend.at[it, pl.ds(p, 3)], trecv.at[it, pl.ds(3 * p, 3)], tplane_sem.at[it]
         ).start()
+
+        @pl.when(it == 0)
+        def _():
+            set_up()
 
         part = trecv.at[it, pl.ds(0, 24)]
         pltpu.make_async_copy(part, part, tplane_sem.at[it]).wait()

time: 61.5 us -> 58.3 us (0.948)
  Pallas kernels: 59.2 us -> 56 us
    pallas_call x1, Pallas kernels: 59.2 us -> 56 us  [on_device(): pl.pallas_call(kernel, out_shape=jax.ShapeDtypeStruct((2, F, B), F32), in...]
where the time goes in v4:
time: 58.3 us; the launch traced here: 58 us
  Pallas kernels  56 us (96%)
  local copies, waits for them, and re-layouts  1.35 us (2%)
  between operations  0.64 us (1%)
    pallas_call x1, Pallas kernels, on_device(): pl.pallas_call(kernel, out_shape=jax.ShapeDtypeStruct((2, F, B), F32), in...  56 us
    transpose x1, local copies, waits for them, and re-layouts, on_device(): return (both[0].T, both[1].T)  1.35 us

profile of v4, /device:TPU:1, one launch (start us, length us, event | category | flops | bytes accessed | tf_op | source)
XLA Modules:
  0.0 58.0 jit_solution(4996284066975656693)
XLA Ops:
  0.6 56.0 %shard_map.86 = f32[2,32,80]{2,1,0:T(8,128)} custom-call(f32[32,80]{1,0:T(8,128)} %bitcast.9, f32[32,70400]{1,0:T(8,128)} %blocks_hbm.1, s32[11,32]{1,0:T(8,128)} %columns_hbm.1, s32[1,32]{1,0:T(1,128)} %slot_hbm.1, f32[32,6400]{1,0:T(8,128)} %low_hbm.1, f32[32,6400]{1,0:T(8,128)} %upp_hbm.1, f32[32,6400]{1,0:T(8,128)} %piv_hbm.1), custom_call_target="tpu_custom_call" | custom-call | tf_op jit(solution)/shard_map/pallas_call | solution.py:455
  56.7 1.3 %slice_bitcast_fusion = (f32[80,32]{0,1:T(8,128)}, f32[80,32]{0,1:T(8,128)}) fusion(f32[2,32,80]{2,1,0:T(8,128)} %shard_map.86), kind=kLoop, calls=%fused_computation | loop fusion | bytes 40960 | tf_op jit(solution)/shard_map/transpose | solution.py:508

commit v5 on v4

--- a/solution.py
+++ b/solution.py
@@ -152,10 +152,7 @@
 
     first = [(near(i // 8, 0), plane_at(i % 8)) for i in range(1, 32)]
     second = [(near(0, i), p) for i in range(1, 8)]
-    for i in range(nplane):
-        greet((s_next, plane_at(i)))
-        greet((s_prev, plane_at(i)))
-    for device in first + second:
+    for device in first[:7] + first[7::8] + second + [(s_next, p), (s_prev, p)]:
         greet(device)
 
     for n in range(3):
@@ -196,7 +193,7 @@
 
     lax.fori_loop(0, NGRP, relayout, 0)
 
-    pl.semaphore_wait(barrier, 16 + 31 + 7)
+    pl.semaphore_wait(barrier, 19)
     send_pieces(0)
     gid_copies = []
     for n, to in enumerate(((s, p_next), (s, p_prev), (s_next, p), (s_prev, p))):

time: 58.3 us -> 56.9 us (0.976)
  Pallas kernels: 56 us -> 54.7 us
    pallas_call x1, Pallas kernels: 56 us -> 54.7 us  [on_device(): pl.pallas_call(kernel, out_shape=jax.ShapeDtypeStruct((2, F, B), F32), in...]
where the time goes in v5:
time: 56.9 us; the launch traced here: 56.7 us
  Pallas kernels  54.7 us (96%)
  local copies, waits for them, and re-layouts  1.35 us (2%)
  between operations  0.64 us (1%)
    pallas_call x1, Pallas kernels, on_device(): pl.pallas_call(kernel, out_shape=jax.ShapeDtypeStruct((2, F, B), F32), in...  54.7 us
    transpose x1, local copies, waits for them, and re-layouts, on_device(): return (both[0].T, both[1].T)  1.35 us

profile of v5, /device:TPU:1, one launch (start us, length us, event | category | flops | bytes accessed | tf_op | source)
XLA Modules:
  0.0 56.7 jit_solution(11418534763143413133)
XLA Ops:
  0.6 54.7 %shard_map.86 = f32[2,32,80]{2,1,0:T(8,128)} custom-call(f32[32,80]{1,0:T(8,128)} %bitcast.9, f32[32,70400]{1,0:T(8,128)} %blocks_hbm.1, s32[11,32]{1,0:T(8,128)} %columns_hbm.1, s32[1,32]{1,0:T(1,128)} %slot_hbm.1, f32[32,6400]{1,0:T(8,128)} %low_hbm.1, f32[32,6400]{1,0:T(8,128)} %upp_hbm.1, f32[32,6400]{1,0:T(8,128)} %piv_hbm.1), custom_call_target="tpu_custom_call" | custom-call | tf_op jit(solution)/shard_map/pallas_call | solution.py:452
  55.3 1.3 %slice_bitcast_fusion = (f32[80,32]{0,1:T(8,128)}, f32[80,32]{0,1:T(8,128)}) fusion(f32[2,32,80]{2,1,0:T(8,128)} %shard_map.86), kind=kLoop, calls=%fused_computation | loop fusion | bytes 40960 | tf_op jit(solution)/shard_map/transpose | solution.py:505

commit v6 on v5

--- a/solution.py
+++ b/solution.py
@@ -107,7 +107,7 @@
     rhs_hbm, blocks_hbm, columns_hbm, slot_hbm, low_hbm, upp_hbm, piv_hbm,
     both_ref,
     rhs_ref, columns_ref, slot_ref, slot_smem, blk, flat, tall, lm, pm, pum, kf, zf, rsend, rrecv, zsend, trecv, gid, early_hot, late_hot, xe, xl, acc, acc2, sfull,
-    thi, tlo, smat, square, ga, gb,
+    thi, tlo, smat, cm, dm, ga, gb,
     load_sem, rsend_sem, rrecv_sem, zsend_sem, tplane_sem, tspan_sem, gsend_sem, grecv_sem,
     gas_sem, gar_sem, gbs_sem, gbr_sem,
 ):
@@ -139,7 +139,7 @@
                 blocks_hbm.at[pl.ds(8 * n, 8)], blk.at[pl.ds(8 * n, 8)], load_sem.at[3 + n]
             )
         )
-    for load in loads:
+    for load in loads[:3]:
         load.start()
 
     barrier = pltpu.get_barrier_semaphore()
@@ -181,14 +181,21 @@
 
     for n in range(3):
         loads[n].wait()
+    for load in loads[3:]:
+        load.start()
 
     def relayout(g, _):
         for n in range(3):
-            chunk = flat[n, :, pl.ds(pl.multiple_of(g * SEG, W), SEG)]
+            first_lane = pl.multiple_of(g * SEG, W)
+            tiles = [flat[n, :, pl.ds(first_lane + v * W, W)] for v in range(5)]
             for a in range(8):
-                tall[n, pl.ds(pl.multiple_of((g * 8 + a) * F, F), F), :] = pad_lanes(
-                    chunk[:, a * B : (a + 1) * B]
-                )
+                tile, at = a * B // W, a * B % W
+                row = tiles[tile]
+                if at > W - B:
+                    row = jnp.where(lane < at, tiles[tile + 1], row)
+                if at:
+                    row = pltpu.roll(row, W - at, 1)
+                tall[n, pl.ds(pl.multiple_of((g * 8 + a) * F, F), F), :] = row
         return 0
 
     lax.fori_loop(0, NGRP, relayout, 0)
@@ -210,6 +217,12 @@
     def flip(m):
         return jnp.transpose(jnp.concatenate([m, zeros48], axis=0))[:B]
 
+    def product(a, b):
+        ah, al = split(a[:, :B])
+        bh, bl = split(b)
+        part = bdot(jnp.concatenate([ah, al], axis=0), jnp.concatenate([bh, bl], axis=1))
+        return part[:B, :W] + (part[:B, W:] + part[B:, :W])
+
     def prepare(c, _):
         for n in range(8):
             row = 8 * c + n
@@ -218,9 +231,7 @@
                 return tall[which, pl.ds(row, B, stride=F), :]
 
             low, piv, upp = matrix(0), matrix(1), matrix(2)
-            ph, pl_ = split(piv[:, :B])
-            uh, ul = split(upp)
-            both = bdot(ph, uh) + (bdot(ph, ul) + bdot(pl_, uh))
+            both = product(piv, upp)
             if n % 2 == 0:
                 lm[row], pm[row], pum[row] = flip(low), piv, both
             else:
@@ -229,12 +240,34 @@
 
     lax.fori_loop(0, F // 8, prepare, 0)
 
-    square[...] = jnp.zeros_like(square)
     for it in range(ITERS):
         zsend[it, 0] = jnp.zeros((4, W), F32)
         zsend[it, nplane + 1] = jnp.zeros((4, W), F32)
     thi[...] = jnp.zeros_like(thi)
     tlo[...] = jnp.zeros_like(tlo)
+
+    def carried():
+        def step(i, cs, ds, odd):
+            new_c, new_d = [], []
+            for m in range(2):
+                low = tall[0, pl.ds(m * 16 + 8 + i, B, stride=F), :]
+                c = -product(low, cs[m])
+                upp = pum[m * 16 + 7 - i]
+                d = -product(upp if odd else flip(upp), ds[m])
+                cm[m * 8 + i] = c if odd else flip(c)
+                dm[m * 8 + 7 - i] = d if odd else flip(d)
+                new_c.append(c)
+                new_d.append(d)
+            return new_c, new_d
+
+        def two(n, carry):
+            cs, ds = step(2 * n + 1, *carry, True)
+            return step(2 * n + 2, cs, ds, False)
+
+        cs = [-tall[0, pl.ds(m * 16 + 8, B, stride=F), :] for m in range(2)]
+        ds = [-flip(pum[m * 16 + 7]) for m in range(2)]
+        cs, ds = lax.fori_loop(0, 3, two, (cs, ds))
+        step(7, cs, ds, True)
 
     def set_up():
         for copy in gid_copies:
@@ -295,42 +328,92 @@
 
     def one(it, _):
         pltpu.make_async_copy(rrecv.at[it], rrecv.at[it], rrecv_sem.at[it]).wait()
-        for m in range(2):
-            for c in range(8):
-                square[pl.ds(m * 8 + c, 1), :] = rrecv[it, c, pl.ds(2 * m + 1, 1), :]
-        odd = jnp.transpose(square[...])[:B]
-        ys = [[], []]
-        for j in range(16):
+        diag = iota((B, W), 0) == iota((B, W), 1)
+
+        def to_lanes(column):
+            return jnp.sum(jnp.where(diag, column, 0.0), axis=0, keepdims=True)
+
+        @pl.when(it == 0)
+        def plain():
+            ys = [[], []]
+            for j in range(16):
+                for m in range(2):
+                    row = m * 16 + j
+                    if j == 0:
+                        ys[m].append(rrecv[it, 0, pl.ds(2 * m, 1), :])
+                    elif j % 2:
+                        base = jnp.where(diag, rrecv[it, j // 2, pl.ds(2 * m + 1, 1), :], 0.0)
+                        ys[m].append(
+                            jnp.sum(base - lm[row] * ys[m][j - 1], axis=1, keepdims=True)
+                        )
+                    else:
+                        r = rrecv[it, j // 2, pl.ds(2 * m, 1), :]
+                        ys[m].append(r - jnp.sum(lm[row] * ys[m][j - 1], axis=0, keepdims=True))
+            zs = [None, None]
+            for j in reversed(range(16)):
+                for m in range(2):
+                    row = m * 16 + j
+                    term = pm[row] * ys[m][j]
+                    if j < 15:
+                        term = term - pum[row] * zs[m]
+                    zs[m] = jnp.sum(term, axis=j % 2 == 0 and 1 or 0, keepdims=True)
+                    if j % 2:
+                        zsend[it, j // 2 + 1, pl.ds(2 * m + 1, 1), :] = zs[m]
+                    else:
+                        zsend[it, j // 2 + 1, pl.ds(2 * m, 1), :] = to_lanes(zs[m])
+
+        @pl.when(it > 0)
+        def halves():
+            ys = [[None] * 16 for _ in range(2)]
+            for i in range(8):
+                for j in (i, 8 + i):
+                    for m in range(2):
+                        row = m * 16 + j
+                        if j % 2:
+                            base = jnp.where(diag, rrecv[it, j // 2, pl.ds(2 * m + 1, 1), :], 0.0)
+                            ys[m][j] = jnp.sum(
+                                base - lm[row] * ys[m][j - 1], axis=1, keepdims=True
+                            )
+                        else:
+                            ys[m][j] = rrecv[it, j // 2, pl.ds(2 * m, 1), :]
+                            if i:
+                                ys[m][j] = ys[m][j] - jnp.sum(
+                                    lm[row] * ys[m][j - 1], axis=0, keepdims=True
+                                )
             for m in range(2):
-                row = m * 16 + j
-                if j == 0:
-                    ys[m].append(rrecv[it, 0, pl.ds(2 * m, 1), :])
-                elif j % 2:
-                    idx = m * 8 + j // 2
-                    base = jnp.where(lane == idx, odd, 0.0)
-                    ys[m].append(
-                        jnp.sum(base - lm[row] * ys[m][j - 1], axis=1, keepdims=True)
-                    )
-                else:
-                    r = rrecv[it, j // 2, pl.ds(2 * m, 1), :]
-                    ys[m].append(r - jnp.sum(lm[row] * ys[m][j - 1], axis=0, keepdims=True))
-        zs = [None, None]
-        even = jnp.zeros((B, W), F32)
-        for j in reversed(range(16)):
+                column = ys[m][7]
+                across = to_lanes(column)
+                ys[m][8] = ys[m][8] - jnp.sum(lm[m * 16 + 8] * column, axis=0, keepdims=True)
+                for i in range(1, 8):
+                    if i % 2:
+                        more = jnp.sum(cm[m * 8 + i] * across, axis=1, keepdims=True)
+                    else:
+                        more = jnp.sum(cm[m * 8 + i] * column, axis=0, keepdims=True)
+                    ys[m][8 + i] = ys[m][8 + i] + more
+            zs = [[None] * 16 for _ in range(2)]
+            for i in range(8):
+                for j in (15 - i, 7 - i):
+                    for m in range(2):
+                        term = pm[m * 16 + j] * ys[m][j]
+                        if i:
+                            term = term - pum[m * 16 + j] * zs[m][j + 1]
+                        zs[m][j] = jnp.sum(term, axis=j % 2 == 0 and 1 or 0, keepdims=True)
             for m in range(2):
-                row = m * 16 + j
-                term = pm[row] * ys[m][j]
-                if j < 15:
-                    term = term - pum[row] * zs[m]
-                zs[m] = jnp.sum(term, axis=j % 2 == 0 and 1 or 0, keepdims=True)
-                if j % 2:
-                    zsend[it, j // 2 + 1, pl.ds(2 * m + 1, 1), :] = zs[m]
-                else:
-                    even = jnp.where(lane == m * 8 + j // 2, zs[m], even)
-        even = jnp.transpose(jnp.concatenate([even, zeros48], axis=0))
-        for m in range(2):
-            for c in range(8):
-                zsend[it, c + 1, pl.ds(2 * m, 1), :] = even[m * 8 + c : m * 8 + c + 1]
+                column = zs[m][8]
+                across = to_lanes(column)
+                for j in range(8):
+                    if j == 7:
+                        more = -jnp.sum(pum[m * 16 + 7] * column, axis=0, keepdims=True)
+                    elif j % 2:
+                        more = jnp.sum(dm[m * 8 + j] * column, axis=0, keepdims=True)
+                    else:
+                        more = jnp.sum(dm[m * 8 + j] * across, axis=1, keepdims=True)
+                    zs[m][j] = zs[m][j] + more
+                for j in range(16):
+                    if j % 2:
+                        zsend[it, j // 2 + 1, pl.ds(2 * m + 1, 1), :] = zs[m][j]
+                    else:
+                        zsend[it, j // 2 + 1, pl.ds(2 * m, 1), :] = to_lanes(zs[m][j])
 
         for i in range(nplane):
             to = plane_at(i)
@@ -354,6 +437,7 @@
         @pl.when(it == 0)
         def _():
             set_up()
+            carried()
 
         part = trecv.at[it, pl.ds(0, 24)]
         pltpu.make_async_copy(part, part, tplane_sem.at[it]).wait()
@@ -482,7 +566,8 @@
             pltpu.VMEM((2 * W, SEG), BF16),
             pltpu.VMEM((2 * W, SEG), BF16),
             pltpu.VMEM((SEG, W), BF16),
-            pltpu.VMEM((W, W), F32),
+            pltpu.VMEM((16, B, W), F32),
+            pltpu.VMEM((16, B, W), F32),
             pltpu.VMEM((32, 1, W), F32),
             pltpu.VMEM((8, 1, W), F32),
             dma((11,)),

time: 56.9 us -> 55.5 us (0.975)
  Pallas kernels: 54.7 us -> 53.3 us
    pallas_call x1, Pallas kernels: 54.7 us -> 53.3 us  [on_device(): pl.pallas_call(kernel, out_shape=jax.ShapeDtypeStruct((2, F, B), F32), in...]
where the time goes in v6:
time: 55.5 us; the launch traced here: 55.2 us
  Pallas kernels  53.3 us (96%)
  local copies, waits for them, and re-layouts  1.35 us (2%)
  between operations  0.64 us (1%)
    pallas_call x1, Pallas kernels, on_device(): pl.pallas_call(kernel, out_shape=jax.ShapeDtypeStruct((2, F, B), F32), in...  53.3 us
    transpose x1, local copies, waits for them, and re-layouts, on_device(): return (both[0].T, both[1].T)  1.35 us

profile of v6, /device:TPU:1, one launch (start us, length us, event | category | flops | bytes accessed | tf_op | source)
XLA Modules:
  0.0 55.2 jit_solution(2901256503639100235)
XLA Ops:
  0.6 53.3 %shard_map.86 = f32[2,32,80]{2,1,0:T(8,128)} custom-call(f32[32,80]{1,0:T(8,128)} %bitcast.9, f32[32,70400]{1,0:T(8,128)} %blocks_hbm.1, s32[11,32]{1,0:T(8,128)} %columns_hbm.1, s32[1,32]{1,0:T(1,128)} %slot_hbm.1, f32[32,6400]{1,0:T(8,128)} %low_hbm.1, f32[32,6400]{1,0:T(8,128)} %upp_hbm.1, f32[32,6400]{1,0:T(8,128)} %piv_hbm.1), custom_call_target="tpu_custom_call" | custom-call | tf_op jit(solution)/shard_map/pallas_call | solution.py:536
  53.9 1.3 %slice_bitcast_fusion = (f32[80,32]{0,1:T(8,128)}, f32[80,32]{0,1:T(8,128)}) fusion(f32[2,32,80]{2,1,0:T(8,128)} %shard_map.86), kind=kLoop, calls=%fused_computation | loop fusion | bytes 40960 | tf_op jit(solution)/shard_map/transpose | solution.py:590

commit v7 on v6

--- a/solution.py
+++ b/solution.py
@@ -530,7 +530,7 @@
 
 def on_device(rhs, blocks, columns, line_slot, line_lower, line_upper, pivot_inv):
     vmem = pl.BlockSpec(memory_space=pltpu.VMEM)
-    hbm = pl.BlockSpec(memory_space=pl.ANY)
+    hbm = pl.BlockSpec(memory_space=pltpu.HBM)
     out = jax.ShapeDtypeStruct((F, B), F32)
     dma = pltpu.SemaphoreType.DMA
     both = pl.pallas_call(
@@ -584,9 +584,14 @@
             dma((1,)),
         ],
         compiler_params=pltpu.CompilerParams(
-            collective_id=0, has_side_effects=True, vmem_limit_bytes=60 * 1024 * 1024
+            collective_id=0, has_side_effects=True, vmem_limit_bytes=48 * 1024 * 1024
         ),
-    )(rhs.T, blocks, columns, line_slot, line_lower, line_upper, pivot_inv)
+    )(
+        *(
+            pltpu.with_memory_space_constraint(given, pltpu.HBM)
+            for given in (rhs.T, blocks, columns, line_slot, line_lower, line_upper, pivot_inv)
+        )
+    )
     return both[0].T, both[1].T
 
 

time: 55.5 us -> 54.1 us (0.975)
  local copies, waits for them, and re-layouts: 1.35 us -> 0.61 us
  Pallas kernels: 53.3 us -> 52.6 us
    transpose x1, local copies, waits for them, and re-layouts: 1.35 us -> 0.61 us  [on_device(): return (both[0].T, both[1].T)]
    pallas_call x1, Pallas kernels: 53.3 us -> 52.6 us  [on_device(): pl.pallas_call(kernel, out_shape=jax.ShapeDtypeStruct((2, F, B), F32), in...]
where the time goes in v7:
time: 54.1 us; the launch traced here: 53.9 us
  Pallas kernels  52.6 us (97%)
  between operations  0.64 us (1%)
  local copies, waits for them, and re-layouts  0.61 us (1%)
    pallas_call x1, Pallas kernels, on_device(): pl.pallas_call(kernel, out_shape=jax.ShapeDtypeStruct((2, F, B), F32), in...  52.6 us

profile of v7, /device:TPU:1, one launch (start us, length us, event | category | flops | bytes accessed | tf_op | source)
XLA Modules:
  0.0 53.9 jit_solution(8884430180367849052)
XLA Ops:
  0.6 52.6 %shard_map.86 = f32[2,32,80]{2,1,0:T(8,128)S(1)} custom-call(f32[32,80]{1,0:T(8,128)} %bitcast.9, f32[32,70400]{1,0:T(8,128)} %blocks_hbm.1, s32[11,32]{1,0:T(8,128)} %columns_hbm.1, s32[1,32]{1,0:T(1,128)} %slot_hbm.1, f32[32,6400]{1,0:T(8,128)} %low_hbm.1, f32[32,6400]{1,0:T(8,128)} %upp_hbm.1, f32[32,6400]{1,0:T(8,128)} %piv_hbm.1), custom_call_target="tpu_custom_call" | custom-call | tf_op jit(solution)/shard_map/pallas_call | solution.py:536
  53.3 0.6 %slice_bitcast_fusion = (f32[80,32]{0,1:T(8,128)}, f32[80,32]{0,1:T(8,128)}) fusion(f32[2,32,80]{2,1,0:T(8,128)S(1)} %shard_map.86), kind=kLoop, calls=%fused_computation | loop fusion | bytes 40960 | tf_op jit(solution)/shard_map/transpose | solution.py:595

commit v8 on v7

--- a/solution.py
+++ b/solution.py
@@ -41,6 +41,17 @@
     return jnp.concatenate([x, jnp.zeros((x.shape[0], W - x.shape[1]), x.dtype)], axis=1)
 
 
+def add_rows(x):
+    x = x[:40] + x[40:]
+    last = x[32:]
+    x = x[:16] + x[16:32]
+    return jnp.sum((x[:8] + x[8:]) + last, axis=0, keepdims=True)
+
+
+def add_lanes(x):
+    return jnp.sum(x, axis=1, keepdims=True)
+
+
 def small_solve(factor, target):
     extent = len(target)
     forward_vals = []
@@ -48,13 +59,13 @@
         running = target[row]
         for inner in range(row):
             running = running - factor[row][inner] * forward_vals[inner]
-        forward_vals.append(running / factor[row][row])
+        forward_vals.append(running * factor[row][row])
     backward_vals = [None] * extent
     for row in reversed(range(extent)):
         running = forward_vals[row]
         for inner in range(row + 1, extent):
             running = running - factor[inner][row] * backward_vals[inner]
-        backward_vals[row] = running / factor[row][row]
+        backward_vals[row] = running * factor[row][row]
     return backward_vals
 
 
@@ -67,9 +78,11 @@
                 out = term if out is None else out + term
         return out
 
-    beta = jnp.sqrt(gram[0, 0] + 1e-6)
+    square = gram[0, 0] + 1e-6
+    scale = lax.rsqrt(square)
+    beta = square * scale
     zero = jnp.zeros_like(beta)
-    basis = [[1.0 / beta]]
+    basis = [[scale]]
     h = [[zero] * ITERS for _ in range(ITERS + 1)]
     for step in range(ITERS):
         w = [zero] + basis[step]
@@ -78,8 +91,10 @@
         for i in range(step + 1):
             for n, c in enumerate(basis[i]):
                 w[n] = w[n] - h[i][step] * c
-        h[step + 1][step] = jnp.sqrt(jnp.maximum(inner(w, w), 0.0) + 1e-6)
-        basis.append([c / h[step + 1][step] for c in w])
+        square = jnp.maximum(inner(w, w), 0.0) + 1e-6
+        scale = lax.rsqrt(square)
+        h[step + 1][step] = square * scale
+        basis.append([c * scale for c in w])
     normal = [
         [sum(h[n][i] * h[n][j] for n in range(min(i, j) + 2)) for j in range(ITERS)]
         for i in range(ITERS)
@@ -90,12 +105,12 @@
         diag = normal[j][j]
         for n in range(j):
             diag = diag - factor[j][n] * factor[j][n]
-        factor[j][j] = jnp.sqrt(diag)
+        factor[j][j] = lax.rsqrt(diag)
         for i in range(j + 1, ITERS):
             below = normal[i][j]
             for n in range(j):
                 below = below - factor[i][n] * factor[j][n]
-            factor[i][j] = below / factor[j][j]
+            factor[i][j] = below * factor[j][j]
     y = small_solve(factor, target)
     out = []
     for n in range(ITERS):
@@ -118,8 +133,10 @@
     s_next, s_prev = lax.rem(s + 1, nspan), lax.rem(s + nspan - 1, nspan)
     p_next, p_prev = lax.rem(p + 1, nplane), lax.rem(p + nplane - 1, nplane)
 
+    peers = [lax.rem(p + i, nplane) for i in range(nplane)]
+
     def plane_at(i):
-        return lax.rem(p + i, nplane)
+        return peers[i]
 
     small = []
     for n, (src, dst) in enumerate(
@@ -150,9 +167,10 @@
     def greet(device):
         pl.semaphore_signal(barrier, inc=1, device_id=device, device_id_type=MESH)
 
-    first = [(near(i // 8, 0), plane_at(i % 8)) for i in range(1, 32)]
-    second = [(near(0, i), p) for i in range(1, 8)]
-    for device in first[:7] + first[7::8] + second + [(s_next, p), (s_prev, p)]:
+    far = (4, 3, 5, 2, 6, 1, 7, 0)
+    first = [(near(i, 0), plane_at(n)) for i in (2, 1, 3, 0) for n in far if i or n]
+    second = [(near(0, i), p) for i in far[:7]]
+    for device in first[24:] + first[7:24:8] + second + [(s_next, p), (s_prev, p)]:
         greet(device)
 
     for n in range(3):
@@ -170,7 +188,7 @@
     gid[0] = jnp.broadcast_to(mine, (8, W))
 
     def send_pieces(it):
-        for i in range(1, nplane):
+        for i in far[:7]:
             to = plane_at(i)
             pltpu.make_async_remote_copy(
                 src_ref=rsend.at[it, to], dst_ref=rrecv.at[it, p],
@@ -331,7 +349,7 @@
         diag = iota((B, W), 0) == iota((B, W), 1)
 
         def to_lanes(column):
-            return jnp.sum(jnp.where(diag, column, 0.0), axis=0, keepdims=True)
+            return add_rows(jnp.where(diag, column, 0.0))
 
         @pl.when(it == 0)
         def plain():
@@ -344,11 +362,11 @@
                     elif j % 2:
                         base = jnp.where(diag, rrecv[it, j // 2, pl.ds(2 * m + 1, 1), :], 0.0)
                         ys[m].append(
-                            jnp.sum(base - lm[row] * ys[m][j - 1], axis=1, keepdims=True)
+                            add_lanes(base - lm[row] * ys[m][j - 1])
                         )
                     else:
                         r = rrecv[it, j // 2, pl.ds(2 * m, 1), :]
-                        ys[m].append(r - jnp.sum(lm[row] * ys[m][j - 1], axis=0, keepdims=True))
+                        ys[m].append(r - add_rows(lm[row] * ys[m][j - 1]))
             zs = [None, None]
             for j in reversed(range(16)):
                 for m in range(2):
@@ -356,7 +374,7 @@
                     term = pm[row] * ys[m][j]
                     if j < 15:
                         term = term - pum[row] * zs[m]
-                    zs[m] = jnp.sum(term, axis=j % 2 == 0 and 1 or 0, keepdims=True)
+                    zs[m] = add_lanes(term) if j % 2 == 0 else add_rows(term)
                     if j % 2:
                         zsend[it, j // 2 + 1, pl.ds(2 * m + 1, 1), :] = zs[m]
                     else:
@@ -371,24 +389,20 @@
                         row = m * 16 + j
                         if j % 2:
                             base = jnp.where(diag, rrecv[it, j // 2, pl.ds(2 * m + 1, 1), :], 0.0)
-                            ys[m][j] = jnp.sum(
-                                base - lm[row] * ys[m][j - 1], axis=1, keepdims=True
-                            )
+                            ys[m][j] = add_lanes(base - lm[row] * ys[m][j - 1])
                         else:
                             ys[m][j] = rrecv[it, j // 2, pl.ds(2 * m, 1), :]
                             if i:
-                                ys[m][j] = ys[m][j] - jnp.sum(
-                                    lm[row] * ys[m][j - 1], axis=0, keepdims=True
-                                )
+                                ys[m][j] = ys[m][j] - add_rows(lm[row] * ys[m][j - 1])
             for m in range(2):
                 column = ys[m][7]
                 across = to_lanes(column)
-                ys[m][8] = ys[m][8] - jnp.sum(lm[m * 16 + 8] * column, axis=0, keepdims=True)
+                ys[m][8] = ys[m][8] - add_rows(lm[m * 16 + 8] * column)
                 for i in range(1, 8):
                     if i % 2:
-                        more = jnp.sum(cm[m * 8 + i] * across, axis=1, keepdims=True)
+                        more = add_lanes(cm[m * 8 + i] * across)
                     else:
-                        more = jnp.sum(cm[m * 8 + i] * column, axis=0, keepdims=True)
+                        more = add_rows(cm[m * 8 + i] * column)
                     ys[m][8 + i] = ys[m][8 + i] + more
             zs = [[None] * 16 for _ in range(2)]
             for i in range(8):
@@ -397,17 +411,17 @@
                         term = pm[m * 16 + j] * ys[m][j]
                         if i:
                             term = term - pum[m * 16 + j] * zs[m][j + 1]
-                        zs[m][j] = jnp.sum(term, axis=j % 2 == 0 and 1 or 0, keepdims=True)
+                        zs[m][j] = add_lanes(term) if j % 2 == 0 else add_rows(term)
             for m in range(2):
                 column = zs[m][8]
                 across = to_lanes(column)
                 for j in range(8):
                     if j == 7:
-                        more = -jnp.sum(pum[m * 16 + 7] * column, axis=0, keepdims=True)
+                        more = -add_rows(pum[m * 16 + 7] * column)
                     elif j % 2:
-                        more = jnp.sum(dm[m * 8 + j] * column, axis=0, keepdims=True)
+                        more = add_rows(dm[m * 8 + j] * column)
                     else:
-                        more = jnp.sum(dm[m * 8 + j] * across, axis=1, keepdims=True)
+                        more = add_lanes(dm[m * 8 + j] * across)
                     zs[m][j] = zs[m][j] + more
                 for j in range(16):
                     if j % 2:
@@ -415,7 +429,7 @@
                     else:
                         zsend[it, j // 2 + 1, pl.ds(2 * m, 1), :] = to_lanes(zs[m][j])
 
-        for i in range(nplane):
+        for i in far:
             to = plane_at(i)
             for n, there in enumerate((s_next, s_prev)):
                 pltpu.make_async_remote_copy(
@@ -423,7 +437,7 @@
                     send_sem=zsend_sem.at[it], recv_sem=tspan_sem.at[it],
                     device_id=(there, to), device_id_type=MESH,
                 ).start()
-        for i in range(1, nplane):
+        for i in far[:7]:
             to = plane_at(i)
             pltpu.make_async_remote_copy(
                 src_ref=zsend.at[it, pl.ds(to, 3)], dst_ref=trecv.at[it, pl.ds(3 * p, 3)],

time: 54.1 us -> 53.5 us (0.989)
  no operation moved by 1% of the time
where the time goes in v8:
time: 53.5 us; the launch traced here: 53.4 us
  Pallas kernels  52.1 us (97%)
  between operations  0.64 us (1%)
  local copies, waits for them, and re-layouts  0.61 us (1%)
    pallas_call x1, Pallas kernels, on_device(): pl.pallas_call(kernel, out_shape=jax.ShapeDtypeStruct((2, F, B), F32), in...  52.1 us

profile of v8, /device:TPU:1, one launch (start us, length us, event | category | flops | bytes accessed | tf_op | source)
XLA Modules:
  0.0 53.4 jit_solution(17032097814192346504)
XLA Ops:
  0.6 52.1 %shard_map.86 = f32[2,32,80]{2,1,0:T(8,128)S(1)} custom-call(f32[32,80]{1,0:T(8,128)} %bitcast.9, f32[32,70400]{1,0:T(8,128)} %blocks_hbm.1, s32[11,32]{1,0:T(8,128)} %columns_hbm.1, s32[1,32]{1,0:T(1,128)} %slot_hbm.1, f32[32,6400]{1,0:T(8,128)} %low_hbm.1, f32[32,6400]{1,0:T(8,128)} %upp_hbm.1, f32[32,6400]{1,0:T(8,128)} %piv_hbm.1), custom_call_target="tpu_custom_call" | custom-call | tf_op jit(solution)/shard_map/pallas_call | solution.py:550
  52.8 0.6 %slice_bitcast_fusion = (f32[80,32]{0,1:T(8,128)}, f32[80,32]{0,1:T(8,128)}) fusion(f32[2,32,80]{2,1,0:T(8,128)S(1)} %shard_map.86), kind=kLoop, calls=%fused_computation | loop fusion | bytes 40960 | tf_op jit(solution)/shard_map/transpose | solution.py:609

commit v9 on v8

--- a/solution.py
+++ b/solution.py
@@ -468,7 +468,9 @@
         pltpu.make_async_copy(part, part, tspan_sem.at[it]).wait()
         widen(it, 24, 16)
         hot = late_hot[...]
-        xl[...] = bdot(hot, thi[...]) + bdot(hot, tlo[...])
+        for n in range(0, SEG, 2 * W):
+            w = min(2 * W, SEG - n)
+            xl[:, n : n + w] = bdot(hot, thi[:, n : n + w]) + bdot(hot, tlo[:, n : n + w])
 
         out = None
         for half in range(2):
@@ -559,7 +561,7 @@
             pltpu.SMEM((1, F), jnp.int32),
             pltpu.VMEM((F, NBLK * B * B), F32),
             pltpu.VMEM((3, F, B * B), F32),
-            pltpu.VMEM((3, B * F, W), F32),
+            pltpu.VMEM((3, B * F + F, W), F32),
             pltpu.VMEM((F, B, W), F32),
             pltpu.VMEM((F, B, W), F32),
             pltpu.VMEM((F, B, W), F32),

time: 53.5 us -> 53.5 us (level)
  no operation moved by 1% of the time
where the time goes in v9:
time: 53.5 us; the launch traced here: 53.3 us
  Pallas kernels  52.1 us (97%)
  between operations  0.64 us (1%)
  local copies, waits for them, and re-layouts  0.61 us (1%)
    pallas_call x1, Pallas kernels, on_device(): pl.pallas_call(kernel, out_shape=jax.ShapeDtypeStruct((2, F, B), F32), in...  52.1 us

profile of v9, /device:TPU:1, one launch (start us, length us, event | category | flops | bytes accessed | tf_op | source)
XLA Modules:
  0.0 53.3 jit_solution(12894649818929253861)
XLA Ops:
  0.6 52.1 %shard_map.86 = f32[2,32,80]{2,1,0:T(8,128)S(1)} custom-call(f32[32,80]{1,0:T(8,128)} %bitcast.9, f32[32,70400]{1,0:T(8,128)} %blocks_hbm.1, s32[11,32]{1,0:T(8,128)} %columns_hbm.1, s32[1,32]{1,0:T(1,128)} %slot_hbm.1, f32[32,6400]{1,0:T(8,128)} %low_hbm.1, f32[32,6400]{1,0:T(8,128)} %upp_hbm.1, f32[32,6400]{1,0:T(8,128)} %piv_hbm.1), custom_call_target="tpu_custom_call" | custom-call | tf_op jit(solution)/shard_map/pallas_call | solution.py:552
  52.7 0.6 %slice_bitcast_fusion = (f32[80,32]{0,1:T(8,128)}, f32[80,32]{0,1:T(8,128)}) fusion(f32[2,32,80]{2,1,0:T(8,128)S(1)} %shard_map.86), kind=kLoop, calls=%fused_computation | loop fusion | bytes 40960 | tf_op jit(solution)/shard_map/transpose | solution.py:611
